TPU v7x, 128 devices: a whole 4x4x4 slice. The times are simulated.
128 devices in a mesh: row: 8 (over x_lo, z), col: 16 (over y, x_hi, core).
Axes of the slice: x: 4 (x_hi: 2, x_lo: 2; x = x_hi * 2 + x_lo), y: 4, z: 4, core: 2. Of those that a mesh axis runs over, the one named last changes fastest.
Arguments:
- a_band: bfloat16 [512, 32, 128, 128], P(('row', 'col')), may hold values from -4 to 4
- a_mask: int32 [512, 32], P(('row', 'col')), may hold values 0 or 1
- b_band: bfloat16 [512, 32, 128, 128], P(('row', 'col')), may hold values from -4 to 4
- b_mask: int32 [512, 32], P(('row', 'col')), may hold values 0 or 1
Outputs:
- c_grid: bfloat16 [512, 64, 128, 128], P('row', 'col')
All inputs are finite; a program needn't handle non-finite values. No bound on the sum of `a_mask` or of `b_mask` on one device may be relied on, other than what follows from the above.
Results may differ from a plain program's by a relative error of at most 0.001.
Values may be sent and summed in bfloat16 or wider, within the bound.
A program may use at most 192 MiB of HBM per device.

v0:
```python
import jax
import jax.numpy as jnp
from jax import lax
from jax.sharding import PartitionSpec as P

STEPS = 4


def shifted(value, axis, steps):
    count = lax.axis_size(axis)
    pairs = [(source, (source + steps) % count) for source in range(count)]
    return lax.ppermute(value, axis, pairs)


def local(a_band, a_mask, b_band, b_mask):
    grid_height = lax.axis_size("row")
    grid_width = lax.axis_size("col")
    grid_row = lax.axis_index("row")
    grid_col = lax.axis_index("col")
    rows_dev = a_band.shape[0]
    band_width = a_band.shape[1]
    block_size = a_band.shape[2]
    devices_all = grid_height * grid_width
    blocks_all = rows_dev * devices_all
    half_band = band_width // 2
    slot_count = band_width // grid_width
    grid_rows = blocks_all // grid_height
    owner_index = grid_row * grid_width + grid_col
    left_vals = (a_band * a_mask[:, :, None, None].astype(jnp.bfloat16)).reshape(
        rows_dev * band_width, block_size, block_size
    )
    right_vals = (b_band * b_mask[:, :, None, None].astype(jnp.bfloat16)).reshape(
        rows_dev * band_width, block_size, block_size
    )
    slot_ids = jnp.arange(slot_count, dtype=jnp.int32)
    repeat_rows = max(rows_dev // grid_height, 1)
    dest_row = jnp.arange(grid_height, dtype=jnp.int32)[:, None, None, None]
    dest_col = jnp.arange(grid_width, dtype=jnp.int32)[None, :, None, None]
    repeat_ids = jnp.arange(repeat_rows, dtype=jnp.int32)[None, None, :, None]
    slot_grid = slot_ids[None, None, None, :]
    full_shape = (grid_height, grid_width, repeat_rows, slot_count)

    def pick_slots(residue, values, is_left):
        local_row = (residue - owner_index * rows_dev) % grid_height + grid_height * repeat_ids
        is_valid = jnp.broadcast_to(local_row < rows_dev, full_shape)
        local_row = jnp.minimum(local_row, rows_dev - 1)
        global_row = owner_index * rows_dev + local_row
        if is_left:
            offset_now = (
                dest_col + dest_row - global_row + half_band
            ) % grid_width + grid_width * slot_grid
        else:
            offset_now = (dest_col - global_row + half_band) % grid_width + grid_width * slot_grid
        flat_index = (local_row * band_width + offset_now).reshape(-1)
        picked = jnp.take(values, flat_index, axis=0)
        picked = jnp.where(is_valid.reshape(-1)[:, None, None], picked, jnp.zeros_like(picked))
        return picked.reshape(devices_all, repeat_rows, slot_count, block_size, block_size)

    left_send = pick_slots(dest_row, left_vals, True)
    right_send = pick_slots((dest_row + dest_col) % grid_height, right_vals, False)
    left_got, right_got = (
        lax.all_to_all(left_send, ("row", "col"), split_axis=0, concat_axis=0, tiled=True),
        lax.all_to_all(right_send, ("row", "col"), split_axis=0, concat_axis=0, tiled=True),
    )
    panel_rows = jnp.arange(grid_rows, dtype=jnp.int32)

    def place_rows(first_row, received):
        global_row = first_row + grid_height * panel_rows
        source = global_row // rows_dev
        repeat_index = global_row % rows_dev // grid_height
        flat_got = received.reshape(devices_all * repeat_rows, slot_count, block_size, block_size)
        return jnp.take(flat_got, source * repeat_rows + repeat_index, axis=0)

    left_panel = place_rows(grid_row, left_got)
    right_panel = place_rows((grid_row + grid_col) % grid_height, right_got)
    accumulated = jnp.zeros((grid_rows, 2 * slot_count, block_size, block_size), jnp.float32)
    zero_block = jnp.zeros((grid_rows, block_size, block_size), jnp.float32)
    panel_rows = jnp.arange(grid_rows, dtype=jnp.int32)
    for step_index in range(STEPS):
        panel_id = (grid_row + grid_col + step_index) % grid_width
        rows_here = grid_row + grid_height * panel_rows
        start_left = (panel_id - rows_here + half_band) % grid_width
        inner_rows = (
            rows_here[:, None] + start_left[:, None] + grid_width * slot_ids[None, :] - half_band
        ) % blocks_all
        start_right = (grid_col - inner_rows[:, 0] + half_band) % grid_width
        carry_over = start_left + start_right >= grid_width
        chosen = jnp.take(right_panel, (inner_rows // grid_height).reshape(-1), axis=0)
        chosen = chosen.reshape(grid_rows, slot_count, slot_count, block_size, block_size)
        products = jnp.einsum(
            "mjab,mjxbc->mjxac", left_panel, chosen, preferred_element_type=jnp.float32
        )
        diagonals = []
        for diag_sum in range(2 * slot_count - 1):
            part_sum = zero_block
            for left_slot in range(
                max(0, diag_sum - slot_count + 1), min(slot_count, diag_sum + 1)
            ):
                part_sum = part_sum + products[:, left_slot, diag_sum - left_slot]
            diagonals.append(part_sum)
        lower_part = jnp.stack(diagonals + [zero_block], axis=1)
        upper_part = jnp.stack([zero_block] + diagonals, axis=1)
        accumulated = accumulated + jnp.where(
            carry_over[:, None, None, None], upper_part, lower_part
        )
        if step_index + 1 < STEPS:
            left_panel = shifted(left_panel, "col", -1)
            right_panel = shifted(right_panel, "row", -1)
    return accumulated.astype(jnp.bfloat16)


def solution(mesh):
    return jax.shard_map(
        local,
        mesh=mesh,
        in_specs=(
            P(("row", "col"), None, None, None),
            P(("row", "col"), None),
            P(("row", "col"), None, None, None),
            P(("row", "col"), None),
        ),
        out_specs=P("row", "col", None, None),
        check_vma=False,
    )
```

profile of v0, /device:TPU:1, one launch (start us, length us, event | category | flops | bytes accessed | tf_op | source)
XLA Modules:
  0.0 737.1 jit_solution(4246211893620798502)
XLA Ops:
  0.5 0.7 convert_element_type.11
  1.2 0.1 broadcast_in_dim.100
  1.4 4.5 broadcast_multiply_fusion.1
  5.9 10.9 %gather_fusion = bf16[256,128,128]{2,1,0:T(8,128)(2,1)} fusion(bf16[128,128,128]{2,1,0:T(8,128)(2,1)} %bitcast.88, s32[1024]{0:T(1024)S(1)} %pad_clamp_fusion.7), kind=kCustom, calls=%fused_computation.clone | custom fusion | bytes 16778240 | tf_op jit(solution)/shard_map/jit(_take)/gather | solution.py:55
  16.7 7.7 %select_select_fusion.1 = bf16[256,128,128]{2,1,0:T(8,128)(2,1)} fusion(bf16[256,128,128]{2,1,0:T(8,128)(2,1)} %gather_fusion, pred[256]{0:T(512)(128)(4,1)S(1)} %compare_and_fusion.7, pred[256]{0:T(512)(128)(4,1)S(1)} %broadcast_in_dim.100), kind=kLoop, calls=%fused_computation.40 | loop fusion | flops 8388608 | bytes 16777728 | tf_op jit(solution)/shard_map/jit(_where)/select_n | solution.py:56
  24.5 12.0 %all-to-all-start = ((bf16[128,1,2,128,128]{4,3,2,1,0:T(8,128)(2,1)}), bf16[128,1,2,128,128]{4,3,2,1,0:T(8,128)(2,1)}, u32[]{:S(2)}, u32[]{:S(2)}) async-start(bf16[128,1,2,128,128]{4,3,2,1,0:T(8,128)(2,1)} %bitcast.95), calls=%async_computation | async-start | bytes 16777216 | tf_op jit(solution)/shard_map/all_to_all | solution.py:63
  36.7 0.2 broadcast_in_dim.103
  36.9 4.5 broadcast_multiply_fusion
  41.4 10.8 %gather_fusion.3 = bf16[256,128,128]{2,1,0:T(8,128)(2,1)} fusion(bf16[128,128,128]{2,1,0:T(8,128)(2,1)} %bitcast.89, s32[1024]{0:T(1024)S(1)} %pad_clamp_fusion.4), kind=kCustom, calls=%fused_computation.3.clone | custom fusion | bytes 16778240 | tf_op jit(solution)/shard_map/jit(_take)/gather | solution.py:55
  52.2 7.7 %select_select_fusion = bf16[256,128,128]{2,1,0:T(8,128)(2,1)} fusion(bf16[256,128,128]{2,1,0:T(8,128)(2,1)} %gather_fusion.3, pred[256]{0:T(512)(128)(4,1)S(1)} %compare_and_fusion.4, pred[256]{0:T(512)(128)(4,1)S(1)} %broadcast_in_dim.103), kind=kLoop, calls=%fused_computation.39 | loop fusion | flops 8388608 | bytes 16777728 | tf_op jit(solution)/shard_map/jit(_where)/select_n | solution.py:56
  59.9 80.2 %all-to-all-done = bf16[128,1,2,128,128]{4,3,2,1,0:T(8,128)(2,1)} async-done(((bf16[128,1,2,128,128]{4,3,2,1,0:T(8,128)(2,1)}), bf16[128,1,2,128,128]{4,3,2,1,0:T(8,128)(2,1)}, u32[]{:S(2)}, u32[]{:S(2)}) %all-to-all-start) | async-done | bytes 8388640 | tf_op jit(solution)/shard_map/all_to_all | solution.py:63
  140.1 12.3 %all-to-all-start.1 = ((bf16[128,1,2,128,128]{4,3,2,1,0:T(8,128)(2,1)}), bf16[128,1,2,128,128]{4,3,2,1,0:T(8,128)(2,1)}, u32[]{:S(2)}, u32[]{:S(2)}) async-start(bf16[128,1,2,128,128]{4,3,2,1,0:T(8,128)(2,1)} %bitcast.94), calls=%async_computation.1 | async-start | bytes 16777216 | tf_op jit(solution)/shard_map/all_to_all | solution.py:62
  152.4 6.5 gather_fusion.1
  158.9 4.6 broadcast_select_fusion.5
  163.5 4.2 collective-permute-start
  167.8 88.3 %all-to-all-done.1 = bf16[128,1,2,128,128]{4,3,2,1,0:T(8,128)(2,1)} async-done(((bf16[128,1,2,128,128]{4,3,2,1,0:T(8,128)(2,1)}), bf16[128,1,2,128,128]{4,3,2,1,0:T(8,128)(2,1)}, u32[]{:S(2)}, u32[]{:S(2)}) %all-to-all-start.1) | async-done | bytes 8388640 | tf_op jit(solution)/shard_map/all_to_all | solution.py:62
  256.1 6.5 gather_fusion.4
  262.6 4.6 broadcast_select_fusion.4
  267.1 1.7 collective-permute-start.1
  269.1 0.1 sub.236
  269.3 0.1 sub.230
  269.4 0.1 sub.218
  270.3 70.3 %collective-permute-done = bf16[64,2,128,128]{3,2,1,0:T(8,128)(2,1)} collective-permute-done((bf16[64,2,128,128]{3,2,1,0:T(8,128)(2,1)}, bf16[64,2,128,128]{3,2,1,0:T(8,128)(2,1)}, u32[]{:S(2)}, u32[]{:S(2)}) %collective-permute-start) | collective-permute-done | bytes 4194336 | tf_op jit(solution)/shard_map/ppermute | solution.py:12
  340.7 4.3 collective-permute-start.2
  345.0 8.9 %gather_fusion.2 = bf16[128,2,128,128]{3,2,1,0:T(8,128)(2,1)} fusion(bf16[64,2,128,128]{3,2,1,0:T(8,128)(2,1)} %broadcast_select_fusion.5, s32[1024]{0:T(1024)S(1)} %pad_clamp_fusion.5), kind=kCustom, calls=%fused_computation.2.clone | custom fusion | bytes 16777728 | tf_op jit(solution)/shard_map/jit(_take)/gather | solution.py:88
  353.9 7.6 %broadcast_select_fusion.3 = bf16[128,2,128,128]{3,2,1,0:T(8,128)(2,1)} fusion(bf16[128,2,128,128]{3,2,1,0:T(8,128)(2,1)} %gather_fusion.2, pred[128]{0:T(512)(128)(4,1)S(1)} %get-tuple-element.14), kind=kLoop, calls=%fused_computation.44 | loop fusion | flops 4194304 | bytes 16777344 | tf_op jit(solution)/shard_map/jit(_take)/select_n | solution.py:88
  361.5 67.9 %collective-permute-done.1 = bf16[64,2,128,128]{3,2,1,0:T(8,128)(2,1)} collective-permute-done((bf16[64,2,128,128]{3,2,1,0:T(8,128)(2,1)}, bf16[64,2,128,128]{3,2,1,0:T(8,128)(2,1)}, u32[]{:S(2)}, u32[]{:S(2)}) %collective-permute-start.1) | collective-permute-done | bytes 4194336 | tf_op jit(solution)/shard_map/ppermute | solution.py:12
  429.4 12.7 %convolution_bitcast_fusion = f32[64,2,2,128,128]{3,4,2,1,0:T(8,128)} fusion(bf16[64,2,2,128,128]{4,3,2,1,0:T(8,128)(2,1)} %bitcast.90, bf16[64,2,128,128]{3,2,1,0:T(8,128)(2,1)} %broadcast_select_fusion.4), kind=kOutput, calls=%fused_computation.32 | convolution fusion | flops 1073741824 | bytes 29360128 | tf_op jit(solution)/shard_map/mjab,mjxbc->mjxac/dot_general | solution.py:90
  442.1 6.5 fusion.35
  448.6 7.8 %slice_bitcast_fusion.9 = (f32[64,1,128,128]{2,3,0,1:T(8,128)}, f32[64,1,128,128]{2,3,0,1:T(8,128)}) fusion(f32[64,2,2,128,128]{3,4,2,1,0:T(8,128)} %convolution_bitcast_fusion), kind=kLoop, calls=%fused_computation.65 | loop fusion | bytes 16777216 | tf_op jit(solution)/shard_map/stack;squeeze | solution.py:102
  456.4 8.9 %gather_fusion.5 = bf16[128,2,128,128]{3,2,1,0:T(8,128)(2,1)} fusion(bf16[64,2,128,128]{3,2,1,0:T(8,128)(2,1)} %collective-permute-done, s32[1024]{0:T(1024)S(1)} %pad_clamp_fusion.2), kind=kCustom, calls=%fused_computation.5.clone | custom fusion | bytes 16777728 | tf_op jit(solution)/shard_map/jit(_take)/gather | solution.py:88
  465.4 7.6 %broadcast_select_fusion.2 = bf16[128,2,128,128]{3,2,1,0:T(8,128)(2,1)} fusion(bf16[128,2,128,128]{3,2,1,0:T(8,128)(2,1)} %gather_fusion.5, pred[128]{0:T(512)(128)(4,1)S(1)} %get-tuple-element.12), kind=kLoop, calls=%fused_computation.43 | loop fusion | flops 4194304 | bytes 16777344 | tf_op jit(solution)/shard_map/jit(_take)/select_n | solution.py:88
  473.0 0.2 collective-permute-start.4
  473.1 12.7 %fusion.22 = f32[64,2,2,128,128]{3,4,0,2,1:T(8,128)} fusion(bf16[64,2,2,128,128]{4,3,2,1,0:T(8,128)(2,1)} %bitcast.91, bf16[64,2,128,128]{3,2,1,0:T(8,128)(2,1)} %collective-permute-done.1), kind=kOutput, calls=%fused_computation.45 | convolution fusion | flops 1073741824 | bytes 29360128 | tf_op jit(solution)/shard_map/mjab,mjxbc->mjxac/dot_general | solution.py:90
  485.8 83.1 %collective-permute-done.3 = bf16[64,2,128,128]{3,2,1,0:T(8,128)(2,1)} collective-permute-done((bf16[64,2,128,128]{3,2,1,0:T(8,128)(2,1)}, bf16[64,2,128,128]{3,2,1,0:T(8,128)(2,1)}, u32[]{:S(2)}, u32[]{:S(2)}) %collective-permute-start.3) | collective-permute-done | bytes 4194336 | tf_op jit(solution)/shard_map/ppermute | solution.py:12
  568.9 11.4 %slice_bitcast_fusion.5 = (f32[64,1,128,128]{2,3,0,1:T(8,128)}, f32[64,1,128,128]{2,3,0,1:T(8,128)}, f32[64,1,128,128]{2,3,0,1:T(8,128)}) fusion(f32[64,2,2,128,128]{3,4,0,2,1:T(8,128)} %fusion.22), kind=kLoop, calls=%fused_computation.59 | loop fusion | flops 1048576 | bytes 29360128 | tf_op jit(solution)/shard_map/stack;squeeze | solution.py:102
  580.3 8.9 %gather_fusion.6 = bf16[128,2,128,128]{3,2,1,0:T(8,128)(2,1)} fusion(bf16[64,2,128,128]{3,2,1,0:T(8,128)(2,1)} %collective-permute-done.2, s32[1024]{0:T(1024)S(1)} %pad_clamp_fusion.1), kind=kCustom, calls=%fused_computation.6.clone | custom fusion | bytes 16777728 | tf_op jit(solution)/shard_map/jit(_take)/gather | solution.py:88
  589.3 7.6 %broadcast_select_fusion.1 = bf16[128,2,128,128]{3,2,1,0:T(8,128)(2,1)} fusion(bf16[128,2,128,128]{3,2,1,0:T(8,128)(2,1)} %gather_fusion.6, pred[128]{0:T(512)(128)(4,1)S(1)} %get-tuple-element.10), kind=kLoop, calls=%fused_computation.42 | loop fusion | flops 4194304 | bytes 16777344 | tf_op jit(solution)/shard_map/jit(_take)/select_n | solution.py:88
  596.8 12.7 %fusion.25 = f32[64,2,2,128,128]{3,4,0,2,1:T(8,128)} fusion(bf16[64,2,2,128,128]{4,3,2,1,0:T(8,128)(2,1)} %bitcast.93, bf16[64,2,128,128]{3,2,1,0:T(8,128)(2,1)} %collective-permute-done.3), kind=kOutput, calls=%fused_computation.46 | convolution fusion | flops 1073741824 | bytes 29360128 | tf_op jit(solution)/shard_map/mjab,mjxbc->mjxac/dot_general | solution.py:90
  609.5 11.5 %slice_bitcast_fusion.3 = (f32[64,1,128,128]{2,3,0,1:T(8,128)}, f32[64,1,128,128]{2,3,0,1:T(8,128)}, f32[64,1,128,128]{2,3,0,1:T(8,128)}) fusion(f32[64,2,2,128,128]{3,4,0,2,1:T(8,128)} %fusion.25), kind=kLoop, calls=%fused_computation.55 | loop fusion | flops 1048576 | bytes 29360128 | tf_op jit(solution)/shard_map/stack;squeeze | solution.py:102
  621.0 9.1 %gather_fusion.7 = bf16[128,2,128,128]{3,2,1,0:T(8,128)(2,1)} fusion(bf16[64,2,128,128]{3,2,1,0:T(8,128)(2,1)} %collective-permute-done.4, s32[1024]{0:T(1024)S(1)} %pad_clamp_fusion), kind=kCustom, calls=%fused_computation.7.clone | custom fusion | bytes 16777728 | tf_op jit(solution)/shard_map/jit(_take)/gather | solution.py:88
  630.1 7.6 %broadcast_select_fusion = bf16[128,2,128,128]{3,2,1,0:T(8,128)(2,1)} fusion(bf16[128,2,128,128]{3,2,1,0:T(8,128)(2,1)} %gather_fusion.7, pred[128]{0:T(512)(128)(4,1)S(1)} %get-tuple-element.6), kind=kLoop, calls=%fused_computation.41 | loop fusion | flops 4194304 | bytes 16777344 | tf_op jit(solution)/shard_map/jit(_take)/select_n | solution.py:88
  637.7 21.1 %collective-permute-done.5 = bf16[64,2,128,128]{3,2,1,0:T(8,128)(2,1)} collective-permute-done((bf16[64,2,128,128]{3,2,1,0:T(8,128)(2,1)}, bf16[64,2,128,128]{3,2,1,0:T(8,128)(2,1)}, u32[]{:S(2)}, u32[]{:S(2)}) %collective-permute-start.5) | collective-permute-done | bytes 4194336 | tf_op jit(solution)/shard_map/ppermute | solution.py:12
  658.8 12.7 %fusion.28 = f32[64,2,2,128,128]{3,4,0,2,1:T(8,128)} fusion(bf16[64,2,2,128,128]{4,3,2,1,0:T(8,128)(2,1)} %bitcast.92, bf16[64,2,128,128]{3,2,1,0:T(8,128)(2,1)} %collective-permute-done.5), kind=kOutput, calls=%fused_computation.47 | convolution fusion | flops 1073741824 | bytes 29360128 | tf_op jit(solution)/shard_map/mjab,mjxbc->mjxac/dot_general | solution.py:90
  671.5 11.4 %slice_bitcast_fusion.1 = (f32[64,1,128,128]{2,3,0,1:T(8,128)}, f32[64,1,128,128]{2,3,0,1:T(8,128)}, f32[64,1,128,128]{2,3,0,1:T(8,128)}) fusion(f32[64,2,2,128,128]{3,4,0,2,1:T(8,128)} %fusion.28), kind=kLoop, calls=%fused_computation.51 | loop fusion | flops 1048576 | bytes 29360128 | tf_op jit(solution)/shard_map/stack;squeeze | solution.py:102
  683.0 2.5 broadcast.1006
  685.5 39.4 %fusion.4 = bf16[64,4,128,128]{2,3,0,1:T(8,128)(2,1)} fusion(f32[64,1,128,128]{2,3,0,1:T(8,128)} %broadcast.1006, f32[64,1,128,128]{2,3,0,1:T(8,128)} %get-tuple-element.26, f32[64,1,128,128]{2,3,0,1:T(8,128)} %fusion.35, f32[64,1,128,128]{2,3,0,1:T(8,128)} %get-tuple-element.25, f32[64,1,128,128]{2,3,0,1:T(8,128)} %get-tuple-element.24, ...), kind=kLoop, calls=%fused_computation.20 | loop fusion | flops 134217728 | bytes 62914816 | tf_op jit(solution)/shard_map/convert_element_type | solution.py:109
  724.9 12.0 %copy.33 = bf16[64,4,128,128]{3,2,1,0:T(8,128)(2,1)} copy(bf16[64,4,128,128]{2,3,0,1:T(8,128)(2,1)} %fusion.4) | data formatting | bytes 16777216 | tf_op jit(solution)/shard_map/convert_element_type | solution.py:109
  (51 shorter events, 1.9 us)
Async XLA Ops:
  24.5 12.1 %copy-start = (s32[4,32]{1,0:T(4,128)S(1)}, s32[4,32]{1,0:T(4,128)}, u32[]{:S(2)}) copy-start(s32[4,32]{1,0:T(4,128)} %param.11) | copy-start | bytes 1540
  24.5 115.6 %all-to-all-start = ((bf16[128,1,2,128,128]{4,3,2,1,0:T(8,128)(2,1)}), bf16[128,1,2,128,128]{4,3,2,1,0:T(8,128)(2,1)}, u32[]{:S(2)}, u32[]{:S(2)}) async-start(bf16[128,1,2,128,128]{4,3,2,1,0:T(8,128)(2,1)} %bitcast.95), calls=%async_computation | async-start | bytes 16777216 | tf_op jit(solution)/shard_map/all_to_all | solution.py:63
  140.1 116.0 %all-to-all-start.1 = ((bf16[128,1,2,128,128]{4,3,2,1,0:T(8,128)(2,1)}), bf16[128,1,2,128,128]{4,3,2,1,0:T(8,128)(2,1)}, u32[]{:S(2)}, u32[]{:S(2)}) async-start(bf16[128,1,2,128,128]{4,3,2,1,0:T(8,128)(2,1)} %bitcast.94), calls=%async_computation.1 | async-start | bytes 16777216 | tf_op jit(solution)/shard_map/all_to_all | solution.py:62
  163.5 177.1 %collective-permute-start = (bf16[64,2,128,128]{3,2,1,0:T(8,128)(2,1)}, bf16[64,2,128,128]{3,2,1,0:T(8,128)(2,1)}, u32[]{:S(2)}, u32[]{:S(2)}) collective-permute-start(bf16[64,2,128,128]{3,2,1,0:T(8,128)(2,1)} %broadcast_select_fusion.5), channel_id=1, source_target_pairs={{0,112},{16,0},{32,16},{48,32},{64,48},{80,64},{96,80},{112,96},{1... | collective-permute-start | bytes 12582920 | tf_op jit(solution)/shard_map/ppermute | solution.py:12
  267.1 162.3 %collective-permute-start.1 = (bf16[64,2,128,128]{3,2,1,0:T(8,128)(2,1)}, bf16[64,2,128,128]{3,2,1,0:T(8,128)(2,1)}, u32[]{:S(2)}, u32[]{:S(2)}) collective-permute-start(bf16[64,2,128,128]{3,2,1,0:T(8,128)(2,1)} %broadcast_select_fusion.4), channel_id=1, source_target_pairs={{0,15},{1,0},{2,1},{3,2},{4,3},{5,4},{6,5},{7,6},{8,7},{9,8},{10,9... | collective-permute-start | bytes 12582920 | tf_op jit(solution)/shard_map/ppermute | solution.py:12
  340.7 132.3 %collective-permute-start.2 = (bf16[64,2,128,128]{3,2,1,0:T(8,128)(2,1)}, bf16[64,2,128,128]{3,2,1,0:T(8,128)(2,1)}, u32[]{:S(2)}, u32[]{:S(2)}) collective-permute-start(bf16[64,2,128,128]{3,2,1,0:T(8,128)(2,1)} %collective-permute-done), channel_id=1, source_target_pairs={{0,112},{16,0},{32,16},{48,32},{64,48},{80,64},{96,80},{112,96},{1... | collective-permute-start | bytes 12582920 | tf_op jit(solution)/shard_map/ppermute | solution.py:12
  429.4 139.5 %collective-permute-start.3 = (bf16[64,2,128,128]{3,2,1,0:T(8,128)(2,1)}, bf16[64,2,128,128]{3,2,1,0:T(8,128)(2,1)}, u32[]{:S(2)}, u32[]{:S(2)}) collective-permute-start(bf16[64,2,128,128]{3,2,1,0:T(8,128)(2,1)} %collective-permute-done.1), channel_id=1, source_target_pairs={{0,15},{1,0},{2,1},{3,2},{4,3},{5,4},{6,5},{7,6},{8,7},{9,8},{10,9... | collective-permute-start | bytes 12582920 | tf_op jit(solution)/shard_map/ppermute | solution.py:12
  473.0 148.0 %collective-permute-start.4 = (bf16[64,2,128,128]{3,2,1,0:T(8,128)(2,1)}, bf16[64,2,128,128]{3,2,1,0:T(8,128)(2,1)}, u32[]{:S(2)}, u32[]{:S(2)}) collective-permute-start(bf16[64,2,128,128]{3,2,1,0:T(8,128)(2,1)} %collective-permute-done.2), channel_id=1, source_target_pairs={{0,112},{16,0},{32,16},{48,32},{64,48},{80,64},{96,80},{112,96},{1... | collective-permute-start | bytes 12582920 | tf_op jit(solution)/shard_map/ppermute | solution.py:12
  568.9 89.9 %collective-permute-start.5 = (bf16[64,2,128,128]{3,2,1,0:T(8,128)(2,1)}, bf16[64,2,128,128]{3,2,1,0:T(8,128)(2,1)}, u32[]{:S(2)}, u32[]{:S(2)}) collective-permute-start(bf16[64,2,128,128]{3,2,1,0:T(8,128)(2,1)} %collective-permute-done.3), channel_id=1, source_target_pairs={{0,15},{1,0},{2,1},{3,2},{4,3},{5,4},{6,5},{7,6},{8,7},{9,8},{10,9... | collective-permute-start | bytes 12582920 | tf_op jit(solution)/shard_map/ppermute | solution.py:12
where the time goes:
time: 751 us; the launch traced here: 737 us
  waiting for transfers between devices  411 us (55%)
  other arithmetic  146 us (19%)
  local copies, waits for them, and re-layouts  94.1 us (13%)
  matrix products  50.8 us (7%)
  starting transfers between devices  34.5 us (5%)
    ppermute x6, waiting for transfers between devices, shifted(): return lax.ppermute(value, axis, pairs)  242 us
    all_to_all x1, waiting for transfers between devices, local(): lax.all_to_all(left_send, ('row', 'col'), split_axis=0, concat_axis=0, ti...  88.3 us
    all_to_all x1, waiting for transfers between devices, local(): lax.all_to_all(right_send, ('row', 'col'), split_axis=0, concat_axis=0, t...  80.2 us
    dot_general x4, matrix products, local(): jnp.einsum('mjab,mjxbc->mjxac', left_panel, chosen, preferred_element_typ...  50.8 us
    convert_element_type x1, other arithmetic, local(): return accumulated.astype(jnp.bfloat16)  39.4 us
    gather x4, local copies, waits for them, and re-layouts, local(): jnp.take(right_panel, (inner_rows // grid_height).reshape(-1), axis=0)  35.9 us
    another operation x3, other arithmetic, local(): upper_part = jnp.stack([zero_block] + diagonals, axis=1)  34.3 us
    select_n x4, other arithmetic, local(): jnp.take(right_panel, (inner_rows // grid_height).reshape(-1), axis=0)  30.4 us
  transfers between devices with their start and end apart: 8, of which 6 were waited for; matrix products, arithmetic and copies ran while one was open for 26% of the time, Pallas kernels for 0%

commit v1 on v0

v1 whole, which is shorter than its diff:
```python
import functools

import jax
import jax.numpy as jnp
from jax import lax
from jax.experimental import pallas as pl
from jax.experimental.pallas import tpu as pltpu
from jax.sharding import PartitionSpec as P

MESH = pl.DeviceIdType.MESH
BS = 128
ZORDER = (0, 1, 3, 2)


def coords():
    row, col = lax.axis_index("row"), lax.axis_index("col")
    return row // 4, row % 4, col // 4, (col // 2) % 2, col % 2


def device(x_lo, z, y, x_hi, core):
    return (x_lo * 4 + z, y * 4 + x_hi * 2 + core)


def exchange_kernel(a, b, a1, a2, a3, bs, b1, b2, sems, a1_sem, a2_sem):
    x_lo, z, y, x_hi, core = coords()
    (bs_s, bs_r, az_s, b1_s, b1_r, ax_s, b2_s, b2_r, a3_s, a3_r) = [sems.at[i] for i in range(10)]

    barrier = pltpu.get_barrier_semaphore()
    partners = [
        device(x_lo, (z + dz) % 4, y, x_hi, (core + dc) % 2)
        for dz in range(4) for dc in range(2) if (dz, dc) != (0, 0)
    ] + [
        device((x_lo + dl) % 2, z, (y + dy) % 4, (x_hi + dh) % 2, core)
        for dl in range(2) for dy in range(4) for dh in range(2) if (dl, dy, dh) != (0, 0, 0)
    ]
    for partner in partners:
        pl.semaphore_signal(barrier, inc=1, device_id=partner, device_id_type=MESH)
    pl.semaphore_wait(barrier, len(partners))

    def send(src, dst, send_sem, recv_sem, to):
        pltpu.make_async_remote_copy(
            src_ref=src, dst_ref=dst, send_sem=send_sem, recv_sem=recv_sem,
            device_id=to, device_id_type=MESH,
        ).start()

    def wait_blocks(ref, sem):
        pltpu.make_async_copy(ref, ref, sem).wait()

    sibling = device(x_lo, z, y, x_hi, 1 - core)

    send(b.at[1 - core], bs, bs_s, bs_r, sibling)

    pltpu.make_async_copy(a.at[z, pl.ds(16 * core, 16)], a1.at[z, core], a1_sem.at[0]).start()
    send(a.at[z, pl.ds(16 * (1 - core), 16)], a1.at[z, core], az_s, a1_sem.at[0], sibling)
    for g in (1, 2, 3):
        dz = ZORDER[g]
        to_z = (z + dz) % 4
        back = ZORDER.index((4 - dz) % 4)
        for part in range(4):
            for dc in range(2):
                h = (core + dc) % 2
                send(
                    a.at[to_z, pl.ds(16 * h + 4 * part, 4)],
                    a1.at[z, core, pl.ds(4 * part, 4)],
                    az_s, a1_sem.at[back],
                    device(x_lo, to_z, y, x_hi, h),
                )

    wait_blocks(bs, bs_r)
    for dc in range(2):
        cs = (core + dc) % 2
        source = b.at[core] if dc == 0 else bs
        for dl in range(2):
            to_lo = (x_lo + dl) % 2

            def pair(index, carry, cs=cs, source=source, to_lo=to_lo, dl=dl):
                q, g = index // 6, index % 6
                d = (q + core) % 2 + 2 * g
                near = d - 4 * to_lo
                col = (8 * x_hi + 4 * cs + q - d + 16) % 16
                to_y, to_hi = col // 4, (col // 2) % 2
                keep = jnp.logical_and(to_y == y, to_hi == x_hi) if dl == 0 else None
                valid = jnp.logical_and(near >= 0, near <= 6)
                slot = jnp.clip(near, 0, 6)
                dst = b1.at[slot, x_lo * 4 + y]

                def remote():
                    send(source.at[index], dst, b1_s, b1_r, device(to_lo, z, to_y, to_hi, core))

                if dl == 0:
                    @pl.when(jnp.logical_and(valid, keep))
                    def _():
                        pltpu.make_async_copy(source.at[index], dst, b1_r).start()

                    @pl.when(jnp.logical_and(valid, jnp.logical_not(keep)))
                    def _():
                        remote()
                else:
                    pl.when(valid)(remote)
                return carry

            lax.fori_loop(0, 24, pair, 0)

    def spread(g):
        zs = (z + ZORDER[g]) % 4
        wait_blocks(a1.at[zs], a1_sem.at[g])
        m = x_lo * 32 + zs * 8 + y * 2 + x_hi
        for dl in range(2):
            for dy in range(4):
                for dh in range(2):
                    to_lo, to_y, to_hi = (x_lo + dl) % 2, (y + dy) % 4, (x_hi + dh) % 2
                    to = device(to_lo, z, to_y, to_hi, core)
                    first = (4 * to_y + 2 * to_hi + 8 * x_hi) % 16

                    def put(start, at, count, to=to, to_lo=to_lo, here=(dl, dy, dh) == (0, 0, 0)):
                        src = a1.at[zs, to_lo, pl.ds(start, count)]
                        dst = a2.at[m, pl.ds(at, count)]
                        if here:
                            pltpu.make_async_copy(src, dst, a2_sem.at[g]).start()
                        else:
                            send(src, dst, ax_s, a2_sem.at[g], to)

                    @pl.when(first < 12)
                    def _():
                        put(jnp.minimum(first, 10), 0, 5)

                    @pl.when(first == 12)
                    def _():
                        put(12, 0, 4)
                        put(0, 4, 1)

                    @pl.when(first == 14)
                    def _():
                        put(14, 0, 2)
                        put(0, 2, 3)

    def share(g):
        zs = (z + ZORDER[g]) % 4
        wait_blocks(a2.at[pl.ds(0, 16)], a2_sem.at[g])
        for half in range(2):
            rows = pl.ds(half * 32 + zs * 8, 8)
            send(a2.at[rows, pl.ds(1 - core, 4)], a3.at[rows], a3_s, a3_r, sibling)

    spread(0)
    wait_blocks(b1, b1_r)
    for piece in range(4):
        for dz in (1, 3, 2):
            to_z = (z + dz) % 4
            send(b1.at[to_z + piece], b2.at[z, piece], b2_s, b2_r, device(x_lo, to_z, y, x_hi, core))
    pltpu.make_async_copy(b1.at[pl.ds(z, 4)], b2.at[z], b2_r).start()
    spread(1)
    spread(2)
    share(0)
    spread(3)
    share(1)
    share(2)
    share(3)

    wait_blocks(a3, a3_r)
    wait_blocks(b2, b2_r)
    wait_blocks(bs, bs_s)
    wait_blocks(a3, a3_s)
    wait_blocks(b2.at[pl.ds(0, 3)], b2_s)
    wait_blocks(b1, az_s)
    wait_blocks(a2.at[pl.ds(0, 60)], ax_s)
    col = 4 * y + 2 * x_hi + core
    own = 0
    for near in range(7):
        inner = (col + 4 * x_lo + near) % 16
        own = own + jnp.where(inner // 8 == x_hi, 1, 0)
    for count in range(8):
        @pl.when(own == count)
        def _(count=count):
            wait_blocks(a2.at[pl.ds(0, 56 - count), pl.ds(0, 2)], b1_s)


def exchange(a, b):
    block = (BS, BS)
    hbm = pl.BlockSpec(memory_space=pl.ANY)
    shapes = [(4, 2, 16), (64, 5), (64, 4), (24, 2), (7, 8, 2), (4, 4, 8, 2)]
    return pl.pallas_call(
        exchange_kernel,
        out_shape=[jax.ShapeDtypeStruct(shape + block, jnp.bfloat16) for shape in shapes],
        in_specs=[hbm, hbm],
        out_specs=[hbm] * len(shapes),
        scratch_shapes=[
            pltpu.SemaphoreType.DMA((10,)),
            pltpu.SemaphoreType.DMA((4,)),
            pltpu.SemaphoreType.DMA((4,)),
        ],
        compiler_params=pltpu.CompilerParams(collective_id=0, has_side_effects=True),
        name="exchange",
    )(a, b)


def product_kernel(a2, a3, b2, out, acc):
    x_lo, z, y, x_hi, core = coords()
    col = 4 * y + 2 * x_hi + core
    row = 4 * x_lo + z
    step = pl.program_id(0)
    acc[...] = jnp.zeros_like(acc)
    for odd in range(2):
        for s in range(4):
            offset = (col + s + 8 * odd) % 16
            d = row + s
            carry = jnp.where(jnp.logical_and(offset >= d, d > 0), 1, 0)
            ahead = (8 * odd + row + offset) // 16
            for other in range(2):
                h = core if other == 0 else 1 - core
                left = a2[odd, core + s] if other == 0 else a3[odd, s]
                n = (step + h - 1 + ahead + 32) % 32
                right_ref = b2.at[(n // 4) % 4, s, (n // 16) * 4 + n % 4]
                right = jnp.concatenate([right_ref[0], right_ref[1]], axis=1)
                part = jnp.dot(left, right, preferred_element_type=jnp.float32)
                at = h + carry
                acc[odd, at] += part[:, :BS]
                acc[odd, at + 1] += part[:, BS:]
    out[...] = acc[...].astype(out.dtype)


def product(a2, a3, b2):
    block = (BS, BS)
    return pl.pallas_call(
        product_kernel,
        grid=(32,),
        out_shape=jax.ShapeDtypeStruct((64, 4) + block, jnp.bfloat16),
        in_specs=[
            pl.BlockSpec((2, 5) + block, lambda i: (i, 0, 0, 0)),
            pl.BlockSpec((2, 4) + block, lambda i: (i, 0, 0, 0)),
            pl.BlockSpec(memory_space=pltpu.VMEM),
        ],
        out_specs=pl.BlockSpec((2, 4) + block, lambda i: (i, 0, 0, 0)),
        scratch_shapes=[pltpu.VMEM((2, 4) + block, jnp.float32)],
        compiler_params=pltpu.CompilerParams(vmem_limit_bytes=40 * 2**20),
        name="product",
    )(a2, a3, b2)


def local(a_band, a_mask, b_band, b_mask):
    left = a_band * a_mask[:, :, None, None].astype(jnp.bfloat16)
    right = b_band * b_mask[:, :, None, None].astype(jnp.bfloat16)
    halves = right.reshape(4, 2, 16, BS, BS)
    parities = []
    for parity in range(2):
        slots = []
        for q in range(4):
            for g in range(6):
                d = (q + parity) % 2 + 2 * g
                slots.append(halves[q, :, (16 - d) % 16])
        parities.append(jnp.stack(slots))
    right = jnp.stack(parities)
    _, a2, a3, _, _, b2 = exchange(left, right)
    return product(a2, a3, b2)


def solution(mesh):
    return jax.shard_map(
        local,
        mesh=mesh,
        in_specs=(
            P(("row", "col"), None, None, None),
            P(("row", "col"), None),
            P(("row", "col"), None, None, None),
            P(("row", "col"), None),
        ),
        out_specs=P("row", "col", None, None),
        check_vma=False,
    )
```

time: 751 us -> 253 us (0.34); the launches traced: 737 us -> 252 us
  waiting for transfers between devices: 411 us -> 0 us
  Pallas kernels: 0 us -> 239 us
  other arithmetic: 146 us -> 8.24 us
  local copies, waits for them, and re-layouts: 94.1 us -> 5.19 us
  matrix products: 50.8 us -> 0 us
  starting transfers between devices: 34.5 us -> 0 us
    ppermute x6 -> x0, waiting for transfers between devices: 242 us -> none  [shifted(): return lax.ppermute(value, axis, pairs)]
    pallas_call x0 -> x2, Pallas kernels: none -> 239 us  [the longest x1 204 us: exchange(): pl.pallas_call(exchange_kernel, out_shape=[jax.ShapeDtypeStruct(shape + b...]
    all_to_all x2 -> x0, waiting for transfers between devices: 169 us -> none  [the longest x1 88.3 us: local(): lax.all_to_all(left_send, ('row', 'col'), split_axis=0, concat_axis=0, ti...]
    gather x8 -> x0, local copies, waits for them, and re-layouts: 70.6 us -> none  [the longest x4 35.9 us: local(): jnp.take(right_panel, (inner_rows // grid_height).reshape(-1), axis=0)]
    select_n x14 -> x0, other arithmetic: 55.1 us -> none  [the longest x4 30.4 us: local(): jnp.take(right_panel, (inner_rows // grid_height).reshape(-1), axis=0)]
    dot_general x4 -> x0, matrix products: 50.8 us -> none  [local(): jnp.einsum('mjab,mjxbc->mjxac', left_panel, chosen, preferred_element_typ...]
    convert_element_type x3 -> x2, other arithmetic: 40.1 us -> 1.37 us  [the longest x1 0.68 us: local(): left = a_band * a_mask[:, :, None, None].astype(jnp.bfloat16)]
    another operation x3 -> x1, other arithmetic: 34.3 us -> 1.99 us  [local(): right = jnp.stack(parities)]
  transfers between devices with their start and end apart: 8 -> 0, of which waited for: 6 -> 0; matrix products, arithmetic and copies ran while one was open for 26% -> 0% of each run, Pallas kernels for 0% -> 0%
where the time goes in v1:
time: 253 us; the launch traced here: 252 us
  Pallas kernels  239 us (94%)
  other arithmetic  8.24 us (3%)
  local copies, waits for them, and re-layouts  5.19 us (2%)
    pallas_call x1, Pallas kernels, exchange(): pl.pallas_call(exchange_kernel, out_shape=[jax.ShapeDtypeStruct(shape + b...  204 us
    pallas_call x1, Pallas kernels, product(): pl.pallas_call(product_kernel, grid=(32,), out_shape=jax.ShapeDtypeStruct...  34.6 us
    unnamed x27, local copies, waits for them, and re-layouts  5.15 us

profile of v1, /device:TPU:1, one launch (start us, length us, event | category | flops | bytes accessed | tf_op | source)
XLA Modules:
  0.0 252.2 jit_solution(17589472936226753026)
XLA Ops:
  0.0 0.7 convert_element_type.8
  0.7 0.7 convert_element_type.9
  1.4 2.5 %broadcast_multiply_fusion = bf16[4,32,128,128]{3,2,1,0:T(8,128)(2,1)S(1)} fusion(bf16[4,32,128,128]{3,2,1,0:T(8,128)(2,1)} %param.6, bf16[4,32]{1,0:T(4,128)(2,1)S(1)} %convert_element_type.9), kind=kLoop, calls=%fused_computation.1 | loop fusion | flops 2097152 | bytes 8388864 | tf_op jit(solution)/shard_map/mul | solution.py:241
  4.6 0.0 copy-start.1
  4.6 2.0 pad_maximum_fusion.b
  6.6 1.3 copy-done.1
  7.9 2.4 broadcast_multiply_fusion.1.a
  10.3 203.9 %exchange.1 = (bf16[4,2,16,128,128]{4,3,2,1,0:T(8,128)(2,1)}, bf16[64,5,128,128]{3,2,1,0:T(8,128)(2,1)}, bf16[64,4,128,128]{3,2,1,0:T(8,128)(2,1)}, bf16[24,2,12...) custom-call(bf16[4,32,128,128]{3,2,1,0:T(8,128)(2,1)} %broadcast_multiply_fusio, ...), custom_call_target="tpu_custom_call" | custom-call | tf_op jit(solution)/shard_map/exchange/pallas_call | solution.py:181
  214.2 0.0 copy-start
  214.2 3.4 %copy-done = bf16[64,4,128,128]{3,2,1,0:T(8,128)(2,1)S(1)} copy-done((bf16[64,4,128,128]{3,2,1,0:T(8,128)(2,1)S(1)}, bf16[64,4,128,128]{3,2,1,0:T(8,128)(2,1)}, u32[]{:S(2)}) %copy-start) | copy-done | bytes 8388632
  217.6 34.6 %product.1 = bf16[64,4,128,128]{3,2,1,0:T(8,128)(2,1)} custom-call(bf16[64,5,128,128]{3,2,1,0:T(8,128)(2,1)} %get-tuple-element.8.a2, bf16[64,4,128,128]{3,2,1,0:T(8,128)(2,1)S(1)} %copy-done, bf16[4,4,8,2,128,128]{5,4,3,2,1,0:T(8,128)(2,1)} %get-tuple-element.10.b2), custom_call_target="tpu_custom_call" | custom-call | tf_op jit(solution)/shard_map/product/pallas_call | solution.py:223
  (25 shorter events, 0.5 us)
Async XLA Ops:
  4.6 3.3 %copy-start.1 = (bf16[4,32,128,128]{3,2,1,0:T(8,128)(2,1)S(1)}, bf16[4,32,128,128]{3,2,1,0:T(8,128)(2,1)}, u32[]{:S(2)}) copy-start(bf16[4,32,128,128]{3,2,1,0:T(8,128)(2,1)} %param.4) | copy-start | bytes 12582916
  214.2 3.4 %copy-start = (bf16[64,4,128,128]{3,2,1,0:T(8,128)(2,1)S(1)}, bf16[64,4,128,128]{3,2,1,0:T(8,128)(2,1)}, u32[]{:S(2)}) copy-start(bf16[64,4,128,128]{3,2,1,0:T(8,128)(2,1)} %get-tuple-element.9.a3) | copy-start | bytes 25165828

commit v2 on v1

v2 whole, which is shorter than its diff:
```python
import functools

import jax
import jax.numpy as jnp
from jax import lax
from jax.experimental import pallas as pl
from jax.experimental.pallas import tpu as pltpu
from jax.sharding import PartitionSpec as P

MESH = pl.DeviceIdType.MESH
BS = 128
ZORDER = (0, 1, 3, 2)
GROUP = 4


def coords():
    row, col = lax.axis_index("row"), lax.axis_index("col")
    return row // 4, row % 4, col // 4, (col // 2) % 2, col % 2


def device(x_lo, z, y, x_hi, core):
    return (x_lo * 4 + z, y * 4 + x_hi * 2 + core)


def exchange_kernel(a, b, left, b2, spare, a1, sa, sb, b1, sems, a1_sem, a2_sem, sa_r, b1_r):
    x_lo, z, y, x_hi, core = coords()
    x = 2 * x_hi + x_lo
    (sb_s, sb_r, sa_s, az_s, b1_s, ax_s, b2_s, b2_r, a3_s, a3_r) = [sems.at[i] for i in range(10)]

    barrier = pltpu.get_barrier_semaphore()
    partners = [device(x_lo, (z + dz) % 4, y, x_hi, core) for dz in range(1, 4)] + [
        device((x_lo + dl) % 2, z, (y + dy) % 4, (x_hi + dh) % 2, core)
        for dl in range(2) for dy in range(4) for dh in range(2) if (dl, dy, dh) != (0, 0, 0)
    ] + [device(x_lo, z, y, x_hi, 1 - core)]
    for partner in partners:
        pl.semaphore_signal(barrier, inc=1, device_id=partner, device_id_type=MESH)
    pl.semaphore_wait(barrier, len(partners))

    def send(src, dst, send_sem, recv_sem, to):
        pltpu.make_async_remote_copy(
            src_ref=src, dst_ref=dst, send_sem=send_sem, recv_sem=recv_sem,
            device_id=to, device_id_type=MESH,
        ).start()

    def wait_blocks(ref, sem):
        pltpu.make_async_copy(ref, ref, sem).wait()

    sibling = device(x_lo, z, y, x_hi, 1 - core)

    def half(q, h):
        return a.at[q, pl.ds(16 * h, 16)]

    for q in range(4):
        send(half((z + ZORDER[q]) % 4, 1 - core), sa.at[(z + ZORDER[q]) % 4], sa_s, sa_r.at[q], sibling)
    send(b.at[1 - core], sb.at[core], sb_s, sb_r, sibling)
    pltpu.make_async_copy(b.at[core], sb.at[core], sb_r).start()

    def along(g, source, cs):
        to_z = (z + ZORDER[g]) % 4
        if g == 0:
            pltpu.make_async_copy(source.at[pl.ds(0, 16)], a1.at[z, cs], a1_sem.at[0]).start()
        else:
            back = ZORDER.index((4 - ZORDER[g]) % 4)
            for part in range(4):
                at = pl.ds(4 * part, 4)
                send(source.at[at], a1.at[z, cs, at], az_s, a1_sem.at[back], device(x_lo, to_z, y, x_hi, core))

    for g in (1, 2, 3, 0):
        along(g, half((z + ZORDER[g]) % 4, core), core)
    for g in (0, 1, 2, 3):
        to_z = (z + ZORDER[g]) % 4
        wait_blocks(sa.at[to_z], sa_r.at[g])
        along(g, sa.at[to_z], 1 - core)

    wait_blocks(sb, sb_r)

    def toward(near, carry):
        for dx in range(4):
            for dy in range(4):
                to_x, to_y = (x + dx) % 4, (y + dy) % 4
                to_lo, to_hi = to_x % 2, to_x // 2
                d = near + 4 * to_lo
                inner = (4 * to_y + 2 * to_hi + core + d) % 16

                @pl.when(inner // 8 == x_hi)
                def _(dx=dx, dy=dy, to_lo=to_lo, to_y=to_y, to_hi=to_hi, d=d, inner=inner):
                    src = sb.at[(inner // 4) % 2, 6 * (inner % 4) + d // 2]
                    dst = b1.at[near, x_lo * 4 + y]
                    if (dx, dy) == (0, 0):
                        pltpu.make_async_copy(src, dst, b1_r.at[near]).start()
                    else:
                        send(src, dst, b1_s, b1_r.at[near], device(to_lo, z, to_y, to_hi, core))
        return carry

    lax.fori_loop(0, 7, toward, 0)

    def lift(near):
        wait_blocks(b1.at[near], b1_r.at[near])
        for dz in (1, 3, 2, 0):
            to_z = (z + dz) % 4
            step = near - to_z

            @pl.when(jnp.logical_and(step >= 0, step < 4))
            def _(dz=dz, to_z=to_z, step=step):
                dst = b2.at[z, jnp.clip(step, 0, 3)]
                if dz == 0:
                    pltpu.make_async_copy(b1.at[near], dst, b2_r).start()
                else:
                    send(b1.at[near], dst, b2_s, b2_r, device(x_lo, to_z, y, x_hi, core))

    def spread(g):
        zs = (z + ZORDER[g]) % 4
        wait_blocks(a1.at[zs], a1_sem.at[g])
        m = x_lo * 32 + zs * 8 + y * 2 + x_hi
        def column(index, dst):
            for dx in range(4):
                for dy in range(4):
                    to_x, to_y = (x + dx) % 4, (y + dy) % 4
                    to_lo, to_hi = to_x % 2, to_x // 2
                    src = a1.at[zs, to_lo, (4 * to_y + 2 * to_hi + index + 8 * x_hi) % 16]
                    if (dx, dy) == (0, 0):
                        pltpu.make_async_copy(src, dst, a2_sem.at[g]).start()
                    else:
                        send(src, dst, ax_s, a2_sem.at[g], device(to_lo, z, to_y, to_hi, core))

        def kept(index, carry):
            column(index + core, left.at[core, m, index])
            return carry

        column(4 * (1 - core), spare.at[m])
        lax.fori_loop(0, 4, kept, 0)

    def share(g):
        zs = (z + ZORDER[g]) % 4
        wait_blocks(left.at[0, pl.ds(0, 20)], a2_sem.at[g])
        for half in range(2):
            rows = pl.ds(half * 32 + zs * 8, 8)
            send(spare.at[rows], left.at[core, rows, 3 * (1 - core)], a3_s, a3_r, sibling)
            send(left.at[core, rows, pl.ds(1 - core, 3)], left.at[core, rows, pl.ds(core, 3)], a3_s, a3_r, sibling)

    spread(0)
    lift(0)
    lift(1)
    lift(2)
    spread(1)
    lift(3)
    lift(4)
    spread(2)
    lift(5)
    lift(6)
    share(0)
    spread(3)
    share(1)
    share(2)
    share(3)

    wait_blocks(left.at[0], a3_r)
    wait_blocks(b2, b2_r)
    wait_blocks(sb.at[0], sb_s)
    wait_blocks(sa, sa_s)
    wait_blocks(left.at[0], a3_s)
    wait_blocks(b2.at[pl.ds(0, 3)], b2_s)
    wait_blocks(left.at[0, pl.ds(0, 24)], az_s)
    wait_blocks(left.at[0, pl.ds(0, 60)], ax_s)
    wait_blocks(left.at[0, pl.ds(0, 15)], ax_s)
    col = 4 * y + 2 * x_hi + core
    own = 0
    for near in range(7):
        inner = (col + 4 * x_lo + near) % 16
        own = own + jnp.where(inner // 8 == x_hi, 1, 0)
    for count in range(8):
        @pl.when(own == count)
        def _(count=count):
            wait_blocks(left.at[0, pl.ds(0, 56 - count), pl.ds(0, 2)], b1_s)


def exchange(a, b):
    block = (BS, BS)
    hbm = pl.BlockSpec(memory_space=pl.ANY)
    shapes = [(2, 64, 4), (4, 4, 8, 2), (64,)]
    stages = [(4, 2, 16), (4, 16), (2, 24, 2), (7, 8, 2)]
    return pl.pallas_call(
        exchange_kernel,
        out_shape=[jax.ShapeDtypeStruct(shape + block, jnp.bfloat16) for shape in shapes],
        in_specs=[hbm, hbm],
        out_specs=[hbm] * len(shapes),
        scratch_shapes=[pltpu.VMEM(stage + block, jnp.bfloat16) for stage in stages] + [
            pltpu.SemaphoreType.DMA((10,)),
            pltpu.SemaphoreType.DMA((4,)),
            pltpu.SemaphoreType.DMA((4,)),
            pltpu.SemaphoreType.DMA((4,)),
            pltpu.SemaphoreType.DMA((7,)),
        ],
        compiler_params=pltpu.CompilerParams(
            collective_id=0, has_side_effects=True, vmem_limit_bytes=32 * 2**20
        ),
        name="exchange",
    )(a, b)


def product_kernel(left, b2, out, right, sems):
    x_lo, z, y, x_hi, core = coords()
    col = 4 * y + 2 * x_hi + core
    row = 4 * x_lo + z
    i = pl.program_id(0)

    def fetch(n):
        return pltpu.make_async_copy(
            b2.at[(n // 4) % 4, :, (n // 16) * 4 + n % 4], right.at[n, :, pl.ds(1, 2)], sems.at[n]
        )

    def ready(n):
        fetch(n).wait()
        for s in range(4):
            right[n, s, 0] = jnp.zeros((BS, BS), jnp.bfloat16)
            right[n, s, 3] = jnp.zeros((BS, BS), jnp.bfloat16)

    @pl.when(i == 0)
    def _():
        def begin(n, carry):
            fetch((n + 31) % 32).start()
            return carry

        lax.fori_loop(0, 32, begin, 0)
        ready(31)
        ready(0)

    for j in range(1, GROUP + 1):
        n = i * GROUP + j
        pl.when(n < 31)(functools.partial(ready, n))

    for odd in range(2):
        before = None
        for j in range(-1, GROUP):
            weights = []
            for s in range(4):
                offset = (col + s + 8 * odd) % 16
                d = row + s
                first = jnp.where(jnp.logical_and(offset >= d, d > 0), 0, 1)
                n = (i * GROUP + j + (8 * odd + row + offset) // 16 + 32) % 32
                weights.append(jnp.concatenate([right[n, s, first + l] for l in range(3)], axis=1))
            lines = []
            if j >= 0:
                lines.append(jnp.concatenate([left[1, 2 * j + odd, s] for s in range(4)], axis=1))
            if j < GROUP - 1:
                lines.append(jnp.concatenate([left[0, 2 * j + 2 + odd, s] for s in range(4)], axis=1))
            part = jnp.dot(
                jnp.concatenate(lines, axis=0), jnp.concatenate(weights, axis=0), preferred_element_type=jnp.float32
            )
            if j >= 0:
                here = part[:BS]
                sums = [
                    before[:, :BS],
                    before[:, BS:2 * BS] + here[:, :BS],
                    before[:, 2 * BS:] + here[:, BS:2 * BS],
                    here[:, 2 * BS:],
                ]
                for l in range(4):
                    out[2 * j + odd, l] = sums[l].astype(out.dtype)
            before = part[-BS:]


def product(left, b2):
    block = (BS, BS)
    return pl.pallas_call(
        product_kernel,
        grid=(32 // GROUP,),
        out_shape=jax.ShapeDtypeStruct((64, 4) + block, jnp.bfloat16),
        in_specs=[
            pl.BlockSpec((2, 2 * GROUP, 4) + block, lambda i: (0, i, 0, 0, 0)),
            pl.BlockSpec(memory_space=pl.ANY),
        ],
        out_specs=pl.BlockSpec((2 * GROUP, 4) + block, lambda i: (i, 0, 0, 0)),
        scratch_shapes=[pltpu.VMEM((32, 4, 4) + block, jnp.bfloat16), pltpu.SemaphoreType.DMA((32,))],
        compiler_params=pltpu.CompilerParams(vmem_limit_bytes=48 * 2**20),
        name="product",
    )(left, b2)


def local(a_band, a_mask, b_band, b_mask):
    left = a_band * a_mask[:, :, None, None].astype(jnp.bfloat16)
    right = b_band * b_mask[:, :, None, None].astype(jnp.bfloat16)
    halves = right.reshape(4, 2, 16, BS, BS)
    parities = []
    for parity in range(2):
        slots = []
        for q in range(4):
            for g in range(6):
                d = (q + parity) % 2 + 2 * g
                slots.append(halves[q, :, (16 - d) % 16])
        parities.append(jnp.stack(slots))
    right = jnp.stack(parities)
    left, right, _ = exchange(left, right)
    return product(left, right)


def solution(mesh):
    return jax.shard_map(
        local,
        mesh=mesh,
        in_specs=(
            P(("row", "col"), None, None, None),
            P(("row", "col"), None),
            P(("row", "col"), None, None, None),
            P(("row", "col"), None),
        ),
        out_specs=P("row", "col", None, None),
        check_vma=False,
    )
```

time: 253 us -> 206 us (0.81)
  Pallas kernels: 239 us -> 195 us
  other arithmetic: 8.24 us -> 4.52 us
    pallas_call x1, Pallas kernels: 204 us -> 178 us  [exchange(): pl.pallas_call(exchange_kernel, out_shape=[jax.ShapeDtypeStruct(shape + b...]
    pallas_call x1, Pallas kernels: 34.6 us -> 17.7 us  [product(): pl.pallas_call(product_kernel, grid=(32 // GROUP,), out_shape=jax.ShapeDt...]
where the time goes in v2:
time: 206 us
  Pallas kernels  195 us (95%)
  local copies, waits for them, and re-layouts  5.63 us (3%)
  other arithmetic  4.52 us (2%)
    pallas_call x1, Pallas kernels, exchange(): pl.pallas_call(exchange_kernel, out_shape=[jax.ShapeDtypeStruct(shape + b...  178 us
    pallas_call x1, Pallas kernels, product(): pl.pallas_call(product_kernel, grid=(32 // GROUP,), out_shape=jax.ShapeDt...  17.7 us
    unnamed x27, local copies, waits for them, and re-layouts  5.59 us

profile of v2, /device:TPU:1, one launch (start us, length us, event | category | flops | bytes accessed | tf_op | source)
XLA Modules:
  0.0 205.9 jit_solution(10061703477174770028)
XLA Ops:
  0.0 0.7 convert_element_type.8
  0.7 0.7 convert_element_type.9
  1.4 2.5 %broadcast_multiply_fusion = bf16[4,32,128,128]{3,2,1,0:T(8,128)(2,1)S(1)} fusion(bf16[4,32,128,128]{3,2,1,0:T(8,128)(2,1)} %param.6, bf16[4,32]{1,0:T(4,128)(2,1)S(1)} %convert_element_type.9), kind=kLoop, calls=%fused_computation.1 | loop fusion | flops 2097152 | bytes 8388864 | tf_op jit(solution)/shard_map/mul | solution.py:282
  4.6 0.0 copy-start.1
  4.6 0.3 pad_maximum_fusion.b
  4.9 1.9 copy-done.1
  6.8 0.3 broadcast_multiply_fusion.1.a
  7.1 177.7 %exchange.1 = (bf16[2,64,4,128,128]{4,3,2,1,0:T(8,128)(2,1)}, bf16[4,4,8,2,128,128]{5,4,3,2,1,0:T(8,128)(2,1)S(1)}, bf16[64,128,128]{2,1,0:T(8,128)(2,1)}) custom-call(bf16[4,32,128,128]{3,2,1,0:T(8,128)(2,1)S(1)} %broadcast_multiply_fusion.1.a, bf16[2,24,2,128,128]{4,3,2,1,0:T(8,128)(2,1)S(1)} %pad_maximum_fusion.b), custom_call_target="tpu_custom_call" | custom-call | tf_op jit(solution)/shard_map/exchange/pallas_call | solution.py:182
  184.9 0.0 copy-start
  184.9 3.3 %copy-done = bf16[4,4,8,2,128,128]{5,4,3,2,1,0:T(8,128)(2,1)} copy-done((bf16[4,4,8,2,128,128]{5,4,3,2,1,0:T(8,128)(2,1)}, bf16[4,4,8,2,128,128]{5,4,3,2,1,0:T(8,128)(2,1)S(1)}, u32[]{:S(2)}) %copy-start) | copy-done | bytes 8388632
  188.1 17.7 %product.1 = bf16[64,4,128,128]{3,2,1,0:T(8,128)(2,1)} custom-call(bf16[2,64,4,128,128]{4,3,2,1,0:T(8,128)(2,1)} %get-tuple-element.7.left, bf16[4,4,8,2,128,128]{5,4,3,2,1,0:T(8,128)(2,1)} %copy-done), custom_call_target="tpu_custom_call" | custom-call | tf_op jit(solution)/shard_map/product/pallas_call | solution.py:265
  (25 shorter events, 0.5 us)
Async XLA Ops:
  4.6 2.2 %copy-start.1 = (bf16[4,32,128,128]{3,2,1,0:T(8,128)(2,1)S(1)}, bf16[4,32,128,128]{3,2,1,0:T(8,128)(2,1)}, u32[]{:S(2)}) copy-start(bf16[4,32,128,128]{3,2,1,0:T(8,128)(2,1)} %param.4) | copy-start | bytes 12582916
  184.9 3.3 %copy-start = (bf16[4,4,8,2,128,128]{5,4,3,2,1,0:T(8,128)(2,1)}, bf16[4,4,8,2,128,128]{5,4,3,2,1,0:T(8,128)(2,1)S(1)}, u32[]{:S(2)}) copy-start(bf16[4,4,8,2,128,128]{5,4,3,2,1,0:T(8,128)(2,1)S(1)} %get-tuple-element.8.b2) | copy-start | bytes 25165828

commit v3 on v2

v3 whole, which is shorter than its diff:
```python
import functools

import jax
import jax.numpy as jnp
from jax import lax
from jax.experimental import pallas as pl
from jax.experimental.pallas import tpu as pltpu
from jax.sharding import PartitionSpec as P

MESH = pl.DeviceIdType.MESH
BS = 128
ZORDER = (0, 1, 3, 2)
GROUP = 8
EXCHANGE_VMEM = 58 * 2**20
PRODUCT_VMEM = 58 * 2**20


def coords():
    row, col = lax.axis_index("row"), lax.axis_index("col")
    return row // 4, row % 4, col // 4, (col // 2) % 2, col % 2


def device(x_lo, z, y, x_hi, core):
    return (x_lo * 4 + z, y * 4 + x_hi * 2 + core)


def exchange_kernel(
    a, am, b, bm, left, b2, ar, br, a1, sa, bp, b1, spare, sems, load_sem, a1_sem, sa_r, b1_r, a2_sem
):
    x_lo, z, y, x_hi, core = coords()
    x = 2 * x_hi + x_lo
    (bp_s, bp_r, sa_s, az_s, b1_s, ax_s, b2_s, b2_r, a3_s, a3_r) = [sems.at[i] for i in range(10)]

    def send(src, dst, send_sem, recv_sem, to):
        pltpu.make_async_remote_copy(
            src_ref=src, dst_ref=dst, send_sem=send_sem, recv_sem=recv_sem,
            device_id=to, device_id_type=MESH,
        ).start()

    def wait_blocks(ref, sem):
        pltpu.make_async_copy(ref, ref, sem).wait()

    def load(g, h):
        q = (z + ZORDER[g]) % 4
        return pltpu.make_async_copy(a.at[q, pl.ds(16 * h, 16)], ar.at[q, h], load_sem.at[2 * g + (h + core) % 2])

    def load_b(q):
        return pltpu.make_async_copy(b.at[q], br.at[q], load_sem.at[8 + q])

    for q in range(4):
        load_b(q).start()
    for h in (1 - core, core):
        for g in range(4):
            load(g, h).start()

    barrier = pltpu.get_barrier_semaphore()
    sibling = device(x_lo, z, y, x_hi, 1 - core)
    partners = [device(x_lo, (z + dz) % 4, y, x_hi, core) for dz in range(1, 4)] + [
        device((x + dx) % 4 % 2, z, (y + dy) % 4, (x + dx) % 4 // 2, core)
        for dx in range(4) for dy in range(4) if (dx, dy) != (0, 0)
    ] + [sibling]
    for partner in partners:
        pl.semaphore_signal(barrier, inc=1, device_id=partner, device_id_type=MESH)

    for q in range(4):
        load_b(q).wait()

    def mask_b(q, carry):
        for d in range(11):
            for h in range(2):
                u = (16 - d) % 16
                keep = bm[q, 16 * h + u].astype(jnp.float32)
                bp[(q + d) % 2, 6 * q + d // 2, h] = (br[q, 16 * h + u].astype(jnp.float32) * keep).astype(jnp.bfloat16)
        bp[(q + 1) % 2, 6 * q + 5] = jnp.zeros((2, BS, BS), jnp.bfloat16)
        return carry

    lax.fori_loop(0, 4, mask_b, 0)
    pl.semaphore_wait(barrier, len(partners))
    send(bp.at[1 - core], bp.at[2], bp_s, bp_r, sibling)

    def mask_a(g, h):
        q = (z + ZORDER[g]) % 4
        load(g, h).wait()

        def one(t, carry):
            keep = am[q, 16 * h + t].astype(jnp.float32)
            ar[q, h, t] = (ar[q, h, t].astype(jnp.float32) * keep).astype(jnp.bfloat16)
            return carry

        lax.fori_loop(0, 16, one, 0)

    for g in range(4):
        mask_a(g, 1 - core)
        q = (z + ZORDER[g]) % 4
        send(ar.at[q, 1 - core], sa.at[q], sa_s, sa_r.at[g], sibling)

    def toward(near, carry, mine):
        for dx in range(4):
            for dy in range(4):
                to_x, to_y = (x + dx) % 4, (y + dy) % 4
                to_lo, to_hi = to_x % 2, to_x // 2
                d = near + 4 * to_lo
                inner = (4 * to_y + 2 * to_hi + core + d) % 16
                wanted = 2 * x_hi + (core if mine else 1 - core)

                @pl.when(inner // 4 == wanted)
                def _(dx=dx, dy=dy, to_lo=to_lo, to_y=to_y, to_hi=to_hi, d=d, inner=inner):
                    src = bp.at[core if mine else 2, 6 * (inner % 4) + d // 2]
                    dst = b1.at[near, x_lo * 4 + y]
                    if (dx, dy) == (0, 0):
                        pltpu.make_async_copy(src, dst, b1_r.at[near]).start()
                    else:
                        send(src, dst, b1_s, b1_r.at[near], device(to_lo, z, to_y, to_hi, core))
        return carry

    lax.fori_loop(0, 7, functools.partial(toward, mine=True), 0)

    def along(g, source, cs):
        to_z = (z + ZORDER[g]) % 4
        if g == 0:
            pltpu.make_async_copy(source, a1.at[z, cs], a1_sem.at[0]).start()
        else:
            back = ZORDER.index((4 - ZORDER[g]) % 4)
            for part in range(4):
                at = pl.ds(4 * part, 4)
                send(source.at[at], a1.at[z, cs, at], az_s, a1_sem.at[back], device(x_lo, to_z, y, x_hi, core))

    for g in (1, 2, 3, 0):
        mask_a(g, core)
        along(g, ar.at[(z + ZORDER[g]) % 4, core], core)
    for g in (0, 1, 2, 3):
        to_z = (z + ZORDER[g]) % 4
        wait_blocks(sa.at[to_z], sa_r.at[g])
        along(g, sa.at[to_z], 1 - core)

    wait_blocks(bp.at[2], bp_r)
    lax.fori_loop(0, 7, functools.partial(toward, mine=False), 0)

    def lift(near):
        wait_blocks(b1.at[near], b1_r.at[near])
        for dz in (1, 3, 2, 0):
            to_z = (z + dz) % 4
            step = near - to_z

            @pl.when(jnp.logical_and(step >= 0, step < 4))
            def _(dz=dz, to_z=to_z, step=step):
                dst = b2.at[z, jnp.clip(step, 0, 3)]
                if dz == 0:
                    pltpu.make_async_copy(b1.at[near], dst, b2_r).start()
                else:
                    send(b1.at[near], dst, b2_s, b2_r, device(x_lo, to_z, y, x_hi, core))

    def spread(g):
        zs = (z + ZORDER[g]) % 4
        wait_blocks(a1.at[zs], a1_sem.at[g])
        m = x_lo * 32 + zs * 8 + y * 2 + x_hi

        def column(index, dst, sem):
            for dx in range(4):
                for dy in range(4):
                    to_x, to_y = (x + dx) % 4, (y + dy) % 4
                    to_lo, to_hi = to_x % 2, to_x // 2
                    src = a1.at[zs, to_lo, (4 * to_y + 2 * to_hi + index + 8 * x_hi) % 16]
                    if (dx, dy) == (0, 0):
                        pltpu.make_async_copy(src, dst, sem).start()
                    else:
                        send(src, dst, ax_s, sem, device(to_lo, z, to_y, to_hi, core))

        def both(index, carry):
            column(index, left.at[core, m, index - core], a2_sem.at[g, index])
            return carry

        column(4 * (1 - core), spare.at[m], a2_sem.at[g, 0])
        lax.fori_loop(1, 4, both, 0)
        column(4 * core, left.at[core, m, 3 * core], a2_sem.at[g, 4])

    def share(g):
        zs = (z + ZORDER[g]) % 4
        for index in range(4):
            wait_blocks(spare.at[pl.ds(0, 16)], a2_sem.at[g, index])
            for half in range(2):
                rows = pl.ds(half * 32 + zs * 8, 8)
                if index == 0:
                    send(spare.at[rows], left.at[core, rows, 3 * (1 - core)], a3_s, a3_r, sibling)
                else:
                    send(
                        left.at[core, rows, index - core], left.at[core, rows, index - 1 + core],
                        a3_s, a3_r, sibling,
                    )

    spread(0)
    lift(0)
    lift(1)
    lift(2)
    spread(1)
    lift(3)
    lift(4)
    spread(2)
    lift(5)
    lift(6)
    share(0)
    spread(3)
    share(1)
    share(2)
    share(3)

    for g in range(4):
        wait_blocks(spare.at[pl.ds(0, 16)], a2_sem.at[g, 4])
    wait_blocks(left.at[0], a3_r)
    wait_blocks(b2, b2_r)
    wait_blocks(bp.at[0], bp_s)
    wait_blocks(sa, sa_s)
    wait_blocks(left.at[0], a3_s)
    wait_blocks(b2.at[pl.ds(0, 3)], b2_s)
    wait_blocks(left.at[0, pl.ds(0, 24)], az_s)
    wait_blocks(left.at[:, pl.ds(0, 50), pl.ds(0, 3)], ax_s)
    col = 4 * y + 2 * x_hi + core
    own = 0
    for near in range(7):
        inner = (col + 4 * x_lo + near) % 16
        own = own + jnp.where(inner // 8 == x_hi, 1, 0)
    for count in range(8):
        @pl.when(own == count)
        def _(count=count):
            wait_blocks(left.at[0, pl.ds(0, 56 - count), pl.ds(0, 2)], b1_s)


def exchange(a, am, b, bm):
    block = (BS, BS)
    hbm = pl.BlockSpec(memory_space=pl.ANY)
    smem = pl.BlockSpec(memory_space=pltpu.SMEM)
    shapes = [(2, 64, 4), (4, 4, 8, 2)]
    stages = [(4, 2, 16), (4, 32), (4, 2, 16), (4, 16), (3, 24, 2), (7, 8, 2), (64,)]
    semaphores = [(10,), (12,), (4,), (4,), (7,), (4, 5)]
    return pl.pallas_call(
        exchange_kernel,
        out_shape=[jax.ShapeDtypeStruct(shape + block, jnp.bfloat16) for shape in shapes],
        in_specs=[hbm, smem, hbm, smem],
        out_specs=[hbm] * len(shapes),
        scratch_shapes=[pltpu.VMEM(stage + block, jnp.bfloat16) for stage in stages]
        + [pltpu.SemaphoreType.DMA(shape) for shape in semaphores],
        compiler_params=pltpu.CompilerParams(
            collective_id=0, has_side_effects=True, vmem_limit_bytes=EXCHANGE_VMEM
        ),
        name="exchange",
    )(a, am, b, bm)


def product_kernel(left, b2, out, right, sems):
    x_lo, z, y, x_hi, core = coords()
    col = 4 * y + 2 * x_hi + core
    row = 4 * x_lo + z
    i = pl.program_id(0)

    def fetch(n):
        return pltpu.make_async_copy(
            b2.at[(n // 4) % 4, :, (n // 16) * 4 + n % 4], right.at[n, :, pl.ds(1, 2)], sems.at[n]
        )

    def ready(n):
        fetch(n).wait()
        for s in range(4):
            right[n, s, 0] = jnp.zeros((BS, BS), jnp.bfloat16)
            right[n, s, 3] = jnp.zeros((BS, BS), jnp.bfloat16)

    @pl.when(i == 0)
    def _():
        def begin(n, carry):
            fetch((n + 31) % 32).start()
            return carry

        lax.fori_loop(0, 32, begin, 0)
        ready(31)
        ready(0)

    for j in range(1, GROUP + 1):
        n = i * GROUP + j
        pl.when(n < 31)(functools.partial(ready, n))

    for odd in range(2):
        before = None
        for j in range(-1, GROUP):
            weights = []
            for s in range(4):
                offset = (col + s + 8 * odd) % 16
                d = row + s
                first = jnp.where(jnp.logical_and(offset >= d, d > 0), 0, 1)
                n = (i * GROUP + j + (8 * odd + row + offset) // 16 + 32) % 32
                weights.append(jnp.concatenate([right[n, s, first + l] for l in range(3)], axis=1))
            lines = []
            if j >= 0:
                lines.append(jnp.concatenate([left[1, 2 * j + odd, s] for s in range(4)], axis=1))
            if j < GROUP - 1:
                lines.append(jnp.concatenate([left[0, 2 * j + 2 + odd, s] for s in range(4)], axis=1))
            part = jnp.dot(
                jnp.concatenate(lines, axis=0), jnp.concatenate(weights, axis=0), preferred_element_type=jnp.float32
            )
            if j >= 0:
                here = part[:BS]
                sums = [
                    before[:, :BS],
                    before[:, BS:2 * BS] + here[:, :BS],
                    before[:, 2 * BS:] + here[:, BS:2 * BS],
                    here[:, 2 * BS:],
                ]
                for l in range(4):
                    out[2 * j + odd, l] = sums[l].astype(out.dtype)
            before = part[-BS:]


def product(left, b2):
    block = (BS, BS)
    return pl.pallas_call(
        product_kernel,
        grid=(32 // GROUP,),
        out_shape=jax.ShapeDtypeStruct((64, 4) + block, jnp.bfloat16),
        in_specs=[
            pl.BlockSpec((2, 2 * GROUP, 4) + block, lambda i: (0, i, 0, 0, 0)),
            pl.BlockSpec(memory_space=pl.ANY),
        ],
        out_specs=pl.BlockSpec((2 * GROUP, 4) + block, lambda i: (i, 0, 0, 0)),
        scratch_shapes=[pltpu.VMEM((32, 4, 4) + block, jnp.bfloat16), pltpu.SemaphoreType.DMA((32,))],
        compiler_params=pltpu.CompilerParams(vmem_limit_bytes=PRODUCT_VMEM),
        name="product",
    )(left, b2)


def local(a_band, a_mask, b_band, b_mask):
    left, right = exchange(a_band, a_mask, b_band, b_mask)
    return product(left, right)


def solution(mesh):
    return jax.shard_map(
        local,
        mesh=mesh,
        in_specs=(
            P(("row", "col"), None, None, None),
            P(("row", "col"), None),
            P(("row", "col"), None, None, None),
            P(("row", "col"), None),
        ),
        out_specs=P("row", "col", None, None),
        check_vma=False,
    )
```

time: 206 us -> 188 us (0.913); the launches traced: 206 us -> 185 us
  Pallas kernels: 195 us -> 185 us
  local copies, waits for them, and re-layouts: 5.63 us -> 0 us
  other arithmetic: 4.52 us -> 0 us
    pallas_call x1, Pallas kernels: 178 us -> 168 us  [exchange(): pl.pallas_call(exchange_kernel, out_shape=[jax.ShapeDtypeStruct(shape + b...]
    unnamed x27 -> x0, local copies, waits for them, and re-layouts: 5.59 us -> none
    mul x2 -> x0, other arithmetic: 2.86 us -> none  [the longest x1 2.52 us: local(): right = b_band * b_mask[:, :, None, None].astype(jnp.bfloat16)]
where the time goes in v3:
time: 188 us; the launch traced here: 185 us
  Pallas kernels  185 us (98%)
    pallas_call x1, Pallas kernels, exchange(): pl.pallas_call(exchange_kernel, out_shape=[jax.ShapeDtypeStruct(shape + b...  168 us
    pallas_call x1, Pallas kernels, product(): pl.pallas_call(product_kernel, grid=(32 // GROUP,), out_shape=jax.ShapeDt...  16.7 us

profile of v3, /device:TPU:1, one launch (start us, length us, event | category | flops | bytes accessed | tf_op | source)
XLA Modules:
  0.0 185.2 jit_solution(13190749615133249069)
XLA Ops:
  0.0 168.4 %exchange.1 = (bf16[2,64,4,128,128]{4,3,2,1,0:T(8,128)(2,1)}, bf16[4,4,8,2,128,128]{5,4,3,2,1,0:T(8,128)(2,1)}) custom-call(bf16[4,32,128,128]{3,2,1,0:T(8,128)(2,1)} %a.1, s32[4,32]{1,0:T(4,128)} %am.1, bf16[4,32,128,128]{3,2,1,0:T(8,128)(2,1)} %b.1, s32[4,32]{1,0:T(4,128)} %bm.1), custom_call_target="tpu_custom_call" | custom-call | tf_op jit(solution)/shard_map/exchange/pallas_call | solution.py:235
  168.4 16.7 %product.1 = bf16[64,4,128,128]{3,2,1,0:T(8,128)(2,1)} custom-call(bf16[2,64,4,128,128]{4,3,2,1,0:T(8,128)(2,1)} %get-tuple-element.7.left, bf16[4,4,8,2,128,128]{5,4,3,2,1,0:T(8,128)(2,1)} %get-tuple-element.8.b2), custom_call_target="tpu_custom_call" | custom-call | tf_op jit(solution)/shard_map/product/pallas_call | solution.py:313

commit v4 on v3

--- a/solution.py
+++ b/solution.py
@@ -25,11 +25,14 @@
 
 
 def exchange_kernel(
-    a, am, b, bm, left, b2, ar, br, a1, sa, bp, b1, spare, sems, load_sem, a1_sem, sa_r, b1_r, a2_sem
+    a, am, b, bm, left, b2, ar, br, a1, ay, sa, bp, b1, spare,
+    sems, load_sem, a1_sem, ay_r, sa_r, b1_r, a2_sem
 ):
     x_lo, z, y, x_hi, core = coords()
     x = 2 * x_hi + x_lo
-    (bp_s, bp_r, sa_s, az_s, b1_s, ax_s, b2_s, b2_r, a3_s, a3_r) = [sems.at[i] for i in range(10)]
+    (bp_s, bp_r, sa_s, az_s, b1_s, ax_s, b2_s, b2_r, a3_s, a3_r, ay_s, relay_s) = [
+        sems.at[i] for i in range(12)
+    ]
 
     def send(src, dst, send_sem, recv_sem, to):
         pltpu.make_async_remote_copy(
@@ -150,36 +153,115 @@
                 else:
                     send(b1.at[near], dst, b2_s, b2_r, device(x_lo, to_z, y, x_hi, core))
 
-    def spread(g):
+    def rows_from(zs, half):
+        return pl.ds(half * 32 + zs * 8, 8)
+
+    def land(index, m, src, sem, to):
+        def put(dst):
+            if to is None:
+                pltpu.make_async_copy(src, dst, sem).start()
+            else:
+                send(src, dst, ax_s, sem, to)
+
+        @pl.when(index == 4 * (1 - core))
+        def _():
+            put(spare.at[m])
+
+        @pl.when(index != 4 * (1 - core))
+        def _():
+            put(left.at[core, m, jnp.clip(index - core, 0, 3)])
+
+    def outer_sem(index, half):
+        return jnp.where(jnp.logical_and(half == 1, index % 4 == 0), 5 + index // 4, index)
+
+    def along_y(g):
         zs = (z + ZORDER[g]) % 4
         wait_blocks(a1.at[zs], a1_sem.at[g])
+        for k in range(3):
+            for cs in range(2):
+                for dy in (1, 3, 2, 0):
+                    to_y = (y + dy) % 4
+                    src = a1.at[zs, cs, (4 * to_y + 2 + k + 8 * x_hi) % 16]
+                    dst = ay.at[zs, y, cs, k]
+                    if dy == 0:
+                        pltpu.make_async_copy(src, dst, ay_r.at[g]).start()
+                    else:
+                        send(src, dst, ay_s, ay_r.at[g], device(x_lo, z, to_y, x_hi, core))
+
+    def along_x(g):
+        zs = (z + ZORDER[g]) % 4
+        wait_blocks(ay.at[zs], ay_r.at[g])
+
+        def one(from_y, carry):
+            m = x_lo * 32 + zs * 8 + from_y * 2 + x_hi
+            for k in (0, 2, 1):
+                for dx in (1, 3, 2, 0):
+                    to_x = (x + dx) % 4
+                    to_lo, to_hi = to_x % 2, to_x // 2
+                    index = k + 2 * (1 - to_hi)
+                    to = None if dx == 0 else device(to_lo, z, y, to_hi, core)
+                    src = ay.at[zs, from_y, to_lo, k]
+                    if k == 1:
+                        land(index, m, src, a2_sem.at[g, index], to)
+                    else:
+                        relayed = jnp.logical_and(x_lo == 1, to_hi == (0 if k == 2 else 1))
+
+                        @pl.when(jnp.logical_not(relayed))
+                        def _(index=index, src=src, to=to):
+                            land(index, m, src, a2_sem.at[g, outer_sem(index, x_lo)], to)
+            return carry
+
+        lax.fori_loop(0, 4, one, 0)
+
+    def direct(g):
+        zs = (z + ZORDER[g]) % 4
         m = x_lo * 32 + zs * 8 + y * 2 + x_hi
 
-        def column(index, dst, sem):
+        def column(outer):
             for dx in range(4):
                 for dy in range(4):
                     to_x, to_y = (x + dx) % 4, (y + dy) % 4
                     to_lo, to_hi = to_x % 2, to_x // 2
+                    index = 4 * to_hi if outer else 1 + 2 * to_hi
                     src = a1.at[zs, to_lo, (4 * to_y + 2 * to_hi + index + 8 * x_hi) % 16]
-                    if (dx, dy) == (0, 0):
-                        pltpu.make_async_copy(src, dst, sem).start()
-                    else:
-                        send(src, dst, ax_s, sem, device(to_lo, z, to_y, to_hi, core))
-
-        def both(index, carry):
-            column(index, left.at[core, m, index - core], a2_sem.at[g, index])
-            return carry
-
-        column(4 * (1 - core), spare.at[m], a2_sem.at[g, 0])
-        lax.fori_loop(1, 4, both, 0)
-        column(4 * core, left.at[core, m, 3 * core], a2_sem.at[g, 4])
+                    to = None if (dx, dy) == (0, 0) else device(to_lo, z, to_y, to_hi, core)
+                    land(index, m, src, a2_sem.at[g, outer_sem(index, x_lo)], to)
+
+        column(False)
+
+        @pl.when(x_lo == 1)
+        def _():
+            column(True)
+
+    def relay(g):
+        zs = (z + ZORDER[g]) % 4
+        for half in range(2):
+            side = (x_hi + half) % 2
+            wait_blocks(spare.at[pl.ds(0, 8)], a2_sem.at[g, outer_sem(4 * (1 - side), half)])
+            to = device(x_lo, z, (y + 1 + 2 * side) % 4, x_hi, core)
+            sem = a2_sem.at[g, outer_sem(4 * side, half)]
+            rows = rows_from(zs, half)
+            mine, other = left.at[core, rows, 3 * core], spare.at[rows]
+
+            @pl.when(core == side)
+            def _(mine=mine, other=other, sem=sem, to=to):
+                send(other, mine, relay_s, sem, to)
+
+            @pl.when(core != side)
+            def _(mine=mine, other=other, sem=sem, to=to):
+                send(mine, other, relay_s, sem, to)
 
     def share(g):
         zs = (z + ZORDER[g]) % 4
-        for index in range(4):
-            wait_blocks(spare.at[pl.ds(0, 16)], a2_sem.at[g, index])
+        for index in (2, 1, 3, 0):
+            if index == 0:
+                for half in range(2):
+                    side = (x_hi + half) % 2
+                    wait_blocks(spare.at[pl.ds(0, 8)], a2_sem.at[g, outer_sem(4 * side, half)])
+            else:
+                wait_blocks(spare.at[pl.ds(0, 16)], a2_sem.at[g, index])
             for half in range(2):
-                rows = pl.ds(half * 32 + zs * 8, 8)
+                rows = rows_from(zs, half)
                 if index == 0:
                     send(spare.at[rows], left.at[core, rows, 3 * (1 - core)], a3_s, a3_r, sibling)
                 else:
@@ -188,24 +270,34 @@
                         a3_s, a3_r, sibling,
                     )
 
-    spread(0)
+    along_y(0)
+    along_x(0)
     lift(0)
     lift(1)
     lift(2)
-    spread(1)
     lift(3)
     lift(4)
-    spread(2)
+    along_y(1)
+    along_y(2)
     lift(5)
     lift(6)
+    along_y(3)
+    along_x(1)
+    direct(0)
+    direct(1)
+    along_x(2)
+    direct(2)
+    direct(3)
+    relay(0)
     share(0)
-    spread(3)
+    along_x(3)
+    relay(1)
     share(1)
+    relay(2)
     share(2)
+    relay(3)
     share(3)
 
-    for g in range(4):
-        wait_blocks(spare.at[pl.ds(0, 16)], a2_sem.at[g, 4])
     wait_blocks(left.at[0], a3_r)
     wait_blocks(b2, b2_r)
     wait_blocks(bp.at[0], bp_s)
@@ -213,7 +305,13 @@
     wait_blocks(left.at[0], a3_s)
     wait_blocks(b2.at[pl.ds(0, 3)], b2_s)
     wait_blocks(left.at[0, pl.ds(0, 24)], az_s)
-    wait_blocks(left.at[:, pl.ds(0, 50), pl.ds(0, 3)], ax_s)
+    wait_blocks(left.at[0, pl.ds(0, 18)], ay_s)
+    for half, count in ((0, 51), (1, 54)):
+        @pl.when(x_lo == half)
+        def _(count=count):
+            wait_blocks(left.at[0, pl.ds(0, count)], ax_s)
+
+    wait_blocks(spare, relay_s)
     col = 4 * y + 2 * x_hi + core
     own = 0
     for near in range(7):
@@ -230,8 +328,8 @@
     hbm = pl.BlockSpec(memory_space=pl.ANY)
     smem = pl.BlockSpec(memory_space=pltpu.SMEM)
     shapes = [(2, 64, 4), (4, 4, 8, 2)]
-    stages = [(4, 2, 16), (4, 32), (4, 2, 16), (4, 16), (3, 24, 2), (7, 8, 2), (64,)]
-    semaphores = [(10,), (12,), (4,), (4,), (7,), (4, 5)]
+    stages = [(4, 2, 16), (4, 32), (4, 2, 16), (4, 4, 2, 3), (4, 16), (3, 24, 2), (7, 8, 2), (64,)]
+    semaphores = [(12,), (12,), (4,), (4,), (4,), (7,), (4, 7)]
     return pl.pallas_call(
         exchange_kernel,
         out_shape=[jax.ShapeDtypeStruct(shape + block, jnp.bfloat16) for shape in shapes],

time: 188 us -> 184 us (0.979); the launches traced: 185 us -> 184 us
  no operation moved by 1% of the time
where the time goes in v4:
time: 184 us
  Pallas kernels  184 us (100%)
    pallas_call x1, Pallas kernels, exchange(): pl.pallas_call(exchange_kernel, out_shape=[jax.ShapeDtypeStruct(shape + b...  167 us
    pallas_call x1, Pallas kernels, product(): pl.pallas_call(product_kernel, grid=(32 // GROUP,), out_shape=jax.ShapeDt...  16.7 us

profile of v4, /device:TPU:1, one launch (start us, length us, event | category | flops | bytes accessed | tf_op | source)
XLA Modules:
  0.0 184.0 jit_solution(10355437228622148755)
XLA Ops:
  0.0 167.2 %exchange.1 = (bf16[2,64,4,128,128]{4,3,2,1,0:T(8,128)(2,1)}, bf16[4,4,8,2,128,128]{5,4,3,2,1,0:T(8,128)(2,1)}) custom-call(bf16[4,32,128,128]{3,2,1,0:T(8,128)(2,1)} %a.1, s32[4,32]{1,0:T(4,128)} %am.1, bf16[4,32,128,128]{3,2,1,0:T(8,128)(2,1)} %b.1, s32[4,32]{1,0:T(4,128)} %bm.1), custom_call_target="tpu_custom_call" | custom-call | tf_op jit(solution)/shard_map/exchange/pallas_call | solution.py:333
  167.2 16.7 %product.1 = bf16[64,4,128,128]{3,2,1,0:T(8,128)(2,1)} custom-call(bf16[2,64,4,128,128]{4,3,2,1,0:T(8,128)(2,1)} %get-tuple-element.7.left, bf16[4,4,8,2,128,128]{5,4,3,2,1,0:T(8,128)(2,1)} %get-tuple-element.8.b2), custom_call_target="tpu_custom_call" | custom-call | tf_op jit(solution)/shard_map/product/pallas_call | solution.py:411

commit v5 on v4

--- a/solution.py
+++ b/solution.py
@@ -10,9 +10,7 @@
 MESH = pl.DeviceIdType.MESH
 BS = 128
 ZORDER = (0, 1, 3, 2)
-GROUP = 8
-EXCHANGE_VMEM = 58 * 2**20
-PRODUCT_VMEM = 58 * 2**20
+VMEM = 58 * 2**20
 
 
 def coords():
@@ -24,13 +22,13 @@
     return (x_lo * 4 + z, y * 4 + x_hi * 2 + core)
 
 
-def exchange_kernel(
-    a, am, b, bm, left, b2, ar, br, a1, ay, sa, bp, b1, spare,
-    sems, load_sem, a1_sem, ay_r, sa_r, b1_r, a2_sem
+def product_kernel(
+    a, am, b, bm, out, left, b2, ar, br, a1, ay, sa, bp, b1, spare,
+    sems, load_sem, a1_sem, ay_r, sa_r, b1_r, a2_sem, near_r, a3_r, out_sem
 ):
     x_lo, z, y, x_hi, core = coords()
     x = 2 * x_hi + x_lo
-    (bp_s, bp_r, sa_s, az_s, b1_s, ax_s, b2_s, b2_r, a3_s, a3_r, ay_s, relay_s) = [
+    (bp_s, bp_r, sa_s, az_s, b1_s, ax_s, b2_s, b2_r, a3_s, ay_s, relay_s, far_s) = [
         sems.at[i] for i in range(12)
     ]
 
@@ -42,6 +40,10 @@
 
     def wait_blocks(ref, sem):
         pltpu.make_async_copy(ref, ref, sem).wait()
+
+    def masked(block, keep):
+        factor = jnp.full((16, BS), keep.astype(jnp.float32)).astype(jnp.bfloat16)
+        return (block.reshape(BS // 16, 16, BS) * factor[None]).reshape(BS, BS)
 
     def load(g, h):
         q = (z + ZORDER[g]) % 4
@@ -72,8 +74,7 @@
         for d in range(11):
             for h in range(2):
                 u = (16 - d) % 16
-                keep = bm[q, 16 * h + u].astype(jnp.float32)
-                bp[(q + d) % 2, 6 * q + d // 2, h] = (br[q, 16 * h + u].astype(jnp.float32) * keep).astype(jnp.bfloat16)
+                bp[(q + d) % 2, 6 * q + d // 2, h] = masked(br[q, 16 * h + u], bm[q, 16 * h + u])
         bp[(q + 1) % 2, 6 * q + 5] = jnp.zeros((2, BS, BS), jnp.bfloat16)
         return carry
 
@@ -86,8 +87,7 @@
         load(g, h).wait()
 
         def one(t, carry):
-            keep = am[q, 16 * h + t].astype(jnp.float32)
-            ar[q, h, t] = (ar[q, h, t].astype(jnp.float32) * keep).astype(jnp.bfloat16)
+            ar[q, h, t] = masked(ar[q, h, t], am[q, 16 * h + t])
             return carry
 
         lax.fori_loop(0, 16, one, 0)
@@ -144,14 +144,40 @@
         for dz in (1, 3, 2, 0):
             to_z = (z + dz) % 4
             step = near - to_z
-
-            @pl.when(jnp.logical_and(step >= 0, step < 4))
+            wanted = jnp.logical_and(step >= 0, step < 4)
+            if dz == 2:
+                wanted = jnp.logical_or(
+                    jnp.logical_and(to_z == 0, near == 0), jnp.logical_and(to_z == 3, near == 6)
+                )
+
+            @pl.when(wanted)
             def _(dz=dz, to_z=to_z, step=step):
-                dst = b2.at[z, jnp.clip(step, 0, 3)]
+                step = jnp.clip(step, 0, 3)
+                dst = b2.at[z, step]
+                to = device(x_lo, to_z, y, x_hi, core)
                 if dz == 0:
                     pltpu.make_async_copy(b1.at[near], dst, b2_r).start()
+                elif dz == 2:
+                    send(b1.at[near], dst, far_s, b2_r, to)
                 else:
-                    send(b1.at[near], dst, b2_s, b2_r, device(x_lo, to_z, y, x_hi, core))
+                    send(b1.at[near], dst, b2_s, near_r.at[dz // 2, step], to)
+
+    def hand_on(way):
+        from_z, to_z = ((z + 3) % 4, (z + 1) % 4) if way == 0 else ((z + 1) % 4, (z + 3) % 4)
+        for step in range(4):
+            wait_blocks(b2.at[0, 0], near_r.at[way, step])
+            near = step + z
+            if way == 0:
+                low = jnp.where(to_z == 0, 3, jnp.where(to_z == 3, 4, to_z))
+                high = jnp.where(to_z == 0, 3, jnp.where(to_z == 3, 5, to_z + 1))
+            else:
+                low = jnp.where(to_z == 0, 1, jnp.where(to_z == 3, 3, to_z + 2))
+                high = jnp.where(to_z == 0, 2, jnp.where(to_z == 3, 3, to_z + 3))
+
+            @pl.when(jnp.logical_and(near >= low, near <= high))
+            def _(step=step, near=near):
+                dst = b2.at[from_z, jnp.clip(near - to_z, 0, 3)]
+                send(b2.at[from_z, step], dst, far_s, b2_r, device(x_lo, to_z, y, x_hi, core))
 
     def rows_from(zs, half):
         return pl.ds(half * 32 + zs * 8, 8)
@@ -263,12 +289,70 @@
             for half in range(2):
                 rows = rows_from(zs, half)
                 if index == 0:
-                    send(spare.at[rows], left.at[core, rows, 3 * (1 - core)], a3_s, a3_r, sibling)
+                    send(spare.at[rows], left.at[core, rows, 3 * (1 - core)], a3_s, a3_r.at[g], sibling)
                 else:
                     send(
                         left.at[core, rows, index - core], left.at[core, rows, index - 1 + core],
-                        a3_s, a3_r, sibling,
+                        a3_s, a3_r.at[g], sibling,
                     )
+
+    col = 4 * y + 2 * x_hi + core
+    row = 4 * x_lo + z
+
+    def result(g, half):
+        slot = 2 * (g % 2) + half
+        first_row = 32 * half + 8 * ((z + ZORDER[g]) % 4)
+        return pltpu.make_async_copy(br.at[slot], out.at[pl.ds(4 * first_row, 32)], out_sem.at[slot])
+
+    def multiply(g):
+        zs = (z + ZORDER[g]) % 4
+        wait_blocks(left.at[0, pl.ds(0, 16)], a3_r.at[g])
+
+        def eight(half, carry):
+            group = 16 * half + 4 * zs
+
+            def four(odd, carry):
+                before = None
+                for j in range(-1, 4):
+                    weights = []
+                    for s in range(4):
+                        offset = (col + s + 8 * odd) % 16
+                        d = row + s
+                        later = jnp.where(jnp.logical_and(offset >= d, d > 0), 0, 1)
+                        n = (group + j + (8 * odd + row + offset) // 16 + 32) % 32
+                        pair = b2.at[(n // 4) % 4, s, (n // 16) * 4 + n % 4]
+                        weights.append(jnp.concatenate(
+                            [masked(pair[0], later), pair[later], masked(pair[1], 1 - later)], axis=1
+                        ))
+                    lines = []
+                    if j >= 0:
+                        lines.append(jnp.concatenate([left[1, 2 * (group + j) + odd, s] for s in range(4)], axis=1))
+                    if j < 3:
+                        lines.append(jnp.concatenate([left[0, 2 * (group + j) + 2 + odd, s] for s in range(4)], axis=1))
+                    part = jnp.dot(
+                        jnp.concatenate(lines, axis=0), jnp.concatenate(weights, axis=0),
+                        preferred_element_type=jnp.float32,
+                    )
+                    if j >= 0:
+                        here = part[:BS]
+                        sums = [
+                            before[:, :BS],
+                            before[:, BS:2 * BS] + here[:, :BS],
+                            before[:, 2 * BS:] + here[:, BS:2 * BS],
+                            here[:, 2 * BS:],
+                        ]
+                        for l in range(4):
+                            br[2 * (g % 2) + half, 4 * (2 * j + odd) + l] = sums[l].astype(br.dtype)
+                    before = part[-BS:]
+                return carry
+
+            if g >= 2:
+                result(g - 2, half).wait()
+            lax.fori_loop(0, 2, four, 0)
+            result(g, half).start()
+            return carry
+
+        lax.fori_loop(0, 2, eight, 0)
 
     along_y(0)
     along_x(0)
@@ -290,20 +374,34 @@
     direct(3)
     relay(0)
     share(0)
+    hand_on(0)
+    hand_on(1)
     along_x(3)
     relay(1)
     share(1)
     relay(2)
     share(2)
+    wait_blocks(b2.at[pl.ds(0, 2)], b2_r)
+    multiply(0)
+    multiply(1)
     relay(3)
     share(3)
-
-    wait_blocks(left.at[0], a3_r)
-    wait_blocks(b2, b2_r)
+    multiply(2)
+    multiply(3)
+
+    for g in (2, 3):
+        for half in range(2):
+            result(g, half).wait()
     wait_blocks(bp.at[0], bp_s)
     wait_blocks(sa, sa_s)
     wait_blocks(left.at[0], a3_s)
-    wait_blocks(b2.at[pl.ds(0, 3)], b2_s)
+    wait_blocks(b2.at[pl.ds(0, 2)], b2_s)
+    inner_z = jnp.logical_or(z == 1, z == 2)
+    for inner, count in ((True, 5), (False, 3)):
+        @pl.when(inner_z == inner)
+        def _(count=count):
+            wait_blocks(b1.at[pl.ds(0, count)], far_s)
+
     wait_blocks(left.at[0, pl.ds(0, 24)], az_s)
     wait_blocks(left.at[0, pl.ds(0, 18)], ay_s)
     for half, count in ((0, 51), (1, 54)):
@@ -312,7 +410,6 @@
             wait_blocks(left.at[0, pl.ds(0, count)], ax_s)
 
     wait_blocks(spare, relay_s)
-    col = 4 * y + 2 * x_hi + core
     own = 0
     for near in range(7):
         inner = (col + 4 * x_lo + near) % 16
@@ -323,109 +420,46 @@
             wait_blocks(left.at[0, pl.ds(0, 56 - count), pl.ds(0, 2)], b1_s)
 
 
-def exchange(a, am, b, bm):
+def product(a, am, b, bm):
     block = (BS, BS)
     hbm = pl.BlockSpec(memory_space=pl.ANY)
     smem = pl.BlockSpec(memory_space=pltpu.SMEM)
-    shapes = [(2, 64, 4), (4, 4, 8, 2)]
-    stages = [(4, 2, 16), (4, 32), (4, 2, 16), (4, 4, 2, 3), (4, 16), (3, 24, 2), (7, 8, 2), (64,)]
-    semaphores = [(12,), (12,), (4,), (4,), (4,), (7,), (4, 7)]
-    return pl.pallas_call(
-        exchange_kernel,
-        out_shape=[jax.ShapeDtypeStruct(shape + block, jnp.bfloat16) for shape in shapes],
+    stages = [
+        (2, 64, 4), (4, 4, 8, 2), (4, 2, 16), (4, 32), (4, 2, 16), (4, 4, 2, 3), (4, 16), (3, 24, 2), (7, 8, 2), (64,)
+    ]
+    semaphores = [(12,), (12,), (4,), (4,), (4,), (7,), (4, 7), (2, 4), (4,), (4,)]
+    out = pl.pallas_call(
+        product_kernel,
+        out_shape=jax.ShapeDtypeStruct((256,) + block, jnp.bfloat16),
         in_specs=[hbm, smem, hbm, smem],
-        out_specs=[hbm] * len(shapes),
+        out_specs=hbm,
         scratch_shapes=[pltpu.VMEM(stage + block, jnp.bfloat16) for stage in stages]
         + [pltpu.SemaphoreType.DMA(shape) for shape in semaphores],
-        compiler_params=pltpu.CompilerParams(
-            collective_id=0, has_side_effects=True, vmem_limit_bytes=EXCHANGE_VMEM
-        ),
+        compiler_params=pltpu.CompilerParams(collective_id=0, has_side_effects=True, vmem_limit_bytes=VMEM),
         name="exchange",
     )(a, am, b, bm)
-
-
-def product_kernel(left, b2, out, right, sems):
-    x_lo, z, y, x_hi, core = coords()
-    col = 4 * y + 2 * x_hi + core
-    row = 4 * x_lo + z
-    i = pl.program_id(0)
-
-    def fetch(n):
-        return pltpu.make_async_copy(
-            b2.at[(n // 4) % 4, :, (n // 16) * 4 + n % 4], right.at[n, :, pl.ds(1, 2)], sems.at[n]
-        )
-
-    def ready(n):
-        fetch(n).wait()
-        for s in range(4):
-            right[n, s, 0] = jnp.zeros((BS, BS), jnp.bfloat16)
-            right[n, s, 3] = jnp.zeros((BS, BS), jnp.bfloat16)
-
-    @pl.when(i == 0)
-    def _():
-        def begin(n, carry):
-            fetch((n + 31) % 32).start()
-            return carry
-
-        lax.fori_loop(0, 32, begin, 0)
-        ready(31)
-        ready(0)
-
-    for j in range(1, GROUP + 1):
-        n = i * GROUP + j
-        pl.when(n < 31)(functools.partial(ready, n))
-
-    for odd in range(2):
-        before = None
-        for j in range(-1, GROUP):
-            weights = []
-            for s in range(4):
-                offset = (col + s + 8 * odd) % 16
-                d = row + s
-                first = jnp.where(jnp.logical_and(offset >= d, d > 0), 0, 1)
-                n = (i * GROUP + j + (8 * odd + row + offset) // 16 + 32) % 32
-                weights.append(jnp.concatenate([right[n, s, first + l] for l in range(3)], axis=1))
-            lines = []
-            if j >= 0:
-                lines.append(jnp.concatenate([left[1, 2 * j + odd, s] for s in range(4)], axis=1))
-            if j < GROUP - 1:
-                lines.append(jnp.concatenate([left[0, 2 * j + 2 + odd, s] for s in range(4)], axis=1))
-            part = jnp.dot(
-                jnp.concatenate(lines, axis=0), jnp.concatenate(weights, axis=0), preferred_element_type=jnp.float32
-            )
-            if j >= 0:
-                here = part[:BS]
-                sums = [
-                    before[:, :BS],
-                    before[:, BS:2 * BS] + here[:, :BS],
-                    before[:, 2 * BS:] + here[:, BS:2 * BS],
-                    here[:, 2 * BS:],
-                ]
-                for l in range(4):
-                    out[2 * j + odd, l] = sums[l].astype(out.dtype)
-            before = part[-BS:]
-
-
-def product(left, b2):
-    block = (BS, BS)
+    return out.reshape((64, 4) + block)
+
+
+def deliver_kernel(src, dst):
+    dst[...] = src[...]
+
+
+def deliver(blocks):
+    spec = pl.BlockSpec((8,) + blocks.shape[1:], lambda i: (i, 0, 0, 0))
     return pl.pallas_call(
-        product_kernel,
-        grid=(32 // GROUP,),
-        out_shape=jax.ShapeDtypeStruct((64, 4) + block, jnp.bfloat16),
-        in_specs=[
-            pl.BlockSpec((2, 2 * GROUP, 4) + block, lambda i: (0, i, 0, 0, 0)),
-            pl.BlockSpec(memory_space=pl.ANY),
-        ],
-        out_specs=pl.BlockSpec((2 * GROUP, 4) + block, lambda i: (i, 0, 0, 0)),
-        scratch_shapes=[pltpu.VMEM((32, 4, 4) + block, jnp.bfloat16), pltpu.SemaphoreType.DMA((32,))],
-        compiler_params=pltpu.CompilerParams(vmem_limit_bytes=PRODUCT_VMEM),
-        name="product",
-    )(left, b2)
+        deliver_kernel,
+        grid=(blocks.shape[0] // 8,),
+        out_shape=jax.ShapeDtypeStruct(blocks.shape, blocks.dtype),
+        in_specs=[spec],
+        out_specs=spec,
+        compiler_params=pltpu.CompilerParams(vmem_limit_bytes=VMEM),
+        name="deliver",
+    )(blocks)
 
 
 def local(a_band, a_mask, b_band, b_mask):
-    left, right = exchange(a_band, a_mask, b_band, b_mask)
-    return product(left, right)
+    return deliver(product(a_band, a_mask, b_band, b_mask))
 
 
 def solution(mesh):

time: 184 us -> 185 us (level)
  no operation moved by 1% of the time
where the time goes in v5:
time: 185 us; the launch traced here: 184 us
  Pallas kernels  184 us (99%)
    pallas_call x1, Pallas kernels, product(): pl.pallas_call(product_kernel, out_shape=jax.ShapeDtypeStruct((256,) + bl...  175 us
    pallas_call x1, Pallas kernels, deliver(): pl.pallas_call(deliver_kernel, grid=(blocks.shape[0] // 8,), out_shape=ja...  8.96 us

profile of v5, /device:TPU:1, one launch (start us, length us, event | category | flops | bytes accessed | tf_op | source)
XLA Modules:
  0.0 183.9 jit_solution(3388180074452069431)
XLA Ops:
  0.0 174.9 %exchange.1 = bf16[256,128,128]{2,1,0:T(8,128)(2,1)} custom-call(bf16[4,32,128,128]{3,2,1,0:T(8,128)(2,1)} %a.1, s32[4,32]{1,0:T(4,128)} %am.1, bf16[4,32,128,128]{3,2,1,0:T(8,128)(2,1)} %b.1, s32[4,32]{1,0:T(4,128)} %bm.1), custom_call_target="tpu_custom_call" | custom-call | tf_op jit(solution)/shard_map/exchange/pallas_call | solution.py:431
  175.0 9.0 %deliver.1 = bf16[64,4,128,128]{3,2,1,0:T(8,128)(2,1)} custom-call(bf16[64,4,128,128]{3,2,1,0:T(8,128)(2,1)} %bitcast.1), custom_call_target="tpu_custom_call" | custom-call | tf_op jit(solution)/shard_map/deliver/pallas_call | solution.py:450

commit v6 on v4

--- a/solution.py
+++ b/solution.py
@@ -43,6 +43,10 @@
     def wait_blocks(ref, sem):
         pltpu.make_async_copy(ref, ref, sem).wait()
 
+    def masked(block, keep):
+        factor = jnp.full((16, BS), keep.astype(jnp.float32)).astype(jnp.bfloat16)
+        return (block.reshape(BS // 16, 16, BS) * factor[None]).reshape(BS, BS)
+
     def load(g, h):
         q = (z + ZORDER[g]) % 4
         return pltpu.make_async_copy(a.at[q, pl.ds(16 * h, 16)], ar.at[q, h], load_sem.at[2 * g + (h + core) % 2])
@@ -72,8 +76,7 @@
         for d in range(11):
             for h in range(2):
                 u = (16 - d) % 16
-                keep = bm[q, 16 * h + u].astype(jnp.float32)
-                bp[(q + d) % 2, 6 * q + d // 2, h] = (br[q, 16 * h + u].astype(jnp.float32) * keep).astype(jnp.bfloat16)
+                bp[(q + d) % 2, 6 * q + d // 2, h] = masked(br[q, 16 * h + u], bm[q, 16 * h + u])
         bp[(q + 1) % 2, 6 * q + 5] = jnp.zeros((2, BS, BS), jnp.bfloat16)
         return carry
 
@@ -86,8 +89,7 @@
         load(g, h).wait()
 
         def one(t, carry):
-            keep = am[q, 16 * h + t].astype(jnp.float32)
-            ar[q, h, t] = (ar[q, h, t].astype(jnp.float32) * keep).astype(jnp.bfloat16)
+            ar[q, h, t] = masked(ar[q, h, t], am[q, 16 * h + t])
             return carry
 
         lax.fori_loop(0, 16, one, 0)
@@ -108,12 +110,13 @@
 
                 @pl.when(inner // 4 == wanted)
                 def _(dx=dx, dy=dy, to_lo=to_lo, to_y=to_y, to_hi=to_hi, d=d, inner=inner):
-                    src = bp.at[core if mine else 2, 6 * (inner % 4) + d // 2]
-                    dst = b1.at[near, x_lo * 4 + y]
-                    if (dx, dy) == (0, 0):
-                        pltpu.make_async_copy(src, dst, b1_r.at[near]).start()
-                    else:
-                        send(src, dst, b1_s, b1_r.at[near], device(to_lo, z, to_y, to_hi, core))
+                    for h in range(2):
+                        src = bp.at[core if mine else 2, 6 * (inner % 4) + d // 2, h]
+                        dst = b1.at[near, x_lo * 4 + y, h]
+                        if (dx, dy) == (0, 0):
+                            pltpu.make_async_copy(src, dst, b1_r.at[near]).start()
+                        else:
+                            send(src, dst, b1_s, b1_r.at[near], device(to_lo, z, to_y, to_hi, core))
         return carry
 
     lax.fori_loop(0, 7, functools.partial(toward, mine=True), 0)
@@ -282,8 +285,8 @@
     lift(5)
     lift(6)
     along_y(3)
+    direct(0)
     along_x(1)
-    direct(0)
     direct(1)
     along_x(2)
     direct(2)

time: 184 us -> 184 us (level)
  no operation moved by 1% of the time
where the time goes in v6:
time: 184 us
  Pallas kernels  184 us (100%)
    pallas_call x1, Pallas kernels, exchange(): pl.pallas_call(exchange_kernel, out_shape=[jax.ShapeDtypeStruct(shape + b...  167 us
    pallas_call x1, Pallas kernels, product(): pl.pallas_call(product_kernel, grid=(32 // GROUP,), out_shape=jax.ShapeDt...  16.7 us

profile of v6, /device:TPU:1, one launch (start us, length us, event | category | flops | bytes accessed | tf_op | source)
XLA Modules:
  0.0 183.9 jit_solution(8918994174521094628)
XLA Ops:
  0.0 167.2 %exchange.1 = (bf16[2,64,4,128,128]{4,3,2,1,0:T(8,128)(2,1)}, bf16[4,4,8,2,128,128]{5,4,3,2,1,0:T(8,128)(2,1)}) custom-call(bf16[4,32,128,128]{3,2,1,0:T(8,128)(2,1)} %a.1, s32[4,32]{1,0:T(4,128)} %am.1, bf16[4,32,128,128]{3,2,1,0:T(8,128)(2,1)} %b.1, s32[4,32]{1,0:T(4,128)} %bm.1), custom_call_target="tpu_custom_call" | custom-call | tf_op jit(solution)/shard_map/exchange/pallas_call | solution.py:336
  167.2 16.7 %product.1 = bf16[64,4,128,128]{3,2,1,0:T(8,128)(2,1)} custom-call(bf16[2,64,4,128,128]{4,3,2,1,0:T(8,128)(2,1)} %get-tuple-element.7.left, bf16[4,4,8,2,128,128]{5,4,3,2,1,0:T(8,128)(2,1)} %get-tuple-element.8.b2), custom_call_target="tpu_custom_call" | custom-call | tf_op jit(solution)/shard_map/product/pallas_call | solution.py:414

commit v7 on v5

--- a/solution.py
+++ b/solution.py
@@ -441,18 +441,37 @@
     return out.reshape((64, 4) + block)
 
 
-def deliver_kernel(src, dst):
-    dst[...] = src[...]
+def deliver_kernel(src, dst, held, in_sem, out_sem):
+    pieces = in_sem.shape[0]
+    rows = src.shape[0] // pieces
+
+    def into(i):
+        at = pl.ds(i * rows, rows)
+        return pltpu.make_async_copy(src.at[at], held.at[at], in_sem.at[i])
+
+    def out_of(i):
+        at = pl.ds(i * rows, rows)
+        return pltpu.make_async_copy(held.at[at], dst.at[at], out_sem.at[i])
+
+    for i in range(pieces):
+        into(i).start()
+    for i in range(pieces):
+        into(i).wait()
+        out_of(i).start()
+    for i in range(pieces):
+        out_of(i).wait()
 
 
 def deliver(blocks):
-    spec = pl.BlockSpec((8,) + blocks.shape[1:], lambda i: (i, 0, 0, 0))
+    hbm = pl.BlockSpec(memory_space=pl.ANY)
     return pl.pallas_call(
         deliver_kernel,
-        grid=(blocks.shape[0] // 8,),
         out_shape=jax.ShapeDtypeStruct(blocks.shape, blocks.dtype),
-        in_specs=[spec],
-        out_specs=spec,
+        in_specs=[hbm],
+        out_specs=hbm,
+        scratch_shapes=[
+            pltpu.VMEM(blocks.shape, blocks.dtype), pltpu.SemaphoreType.DMA((16,)), pltpu.SemaphoreType.DMA((16,))
+        ],
         compiler_params=pltpu.CompilerParams(vmem_limit_bytes=VMEM),
         name="deliver",
     )(blocks)

time: 185 us -> 182 us (0.984)
  Pallas kernels: 184 us -> 182 us
    pallas_call x1, Pallas kernels: 8.96 us -> 6.57 us  [deliver(): pl.pallas_call(deliver_kernel, out_shape=jax.ShapeDtypeStruct(blocks.shap...]
where the time goes in v7:
time: 182 us
  Pallas kernels  182 us (100%)
    pallas_call x1, Pallas kernels, product(): pl.pallas_call(product_kernel, out_shape=jax.ShapeDtypeStruct((256,) + bl...  175 us
    pallas_call x1, Pallas kernels, deliver(): pl.pallas_call(deliver_kernel, out_shape=jax.ShapeDtypeStruct(blocks.shap...  6.57 us

profile of v7, /device:TPU:1, one launch (start us, length us, event | category | flops | bytes accessed | tf_op | source)
XLA Modules:
  0.0 181.5 jit_solution(4795106349100752889)
XLA Ops:
  0.0 174.9 %exchange.1 = bf16[256,128,128]{2,1,0:T(8,128)(2,1)} custom-call(bf16[4,32,128,128]{3,2,1,0:T(8,128)(2,1)} %a.1, s32[4,32]{1,0:T(4,128)} %am.1, bf16[4,32,128,128]{3,2,1,0:T(8,128)(2,1)} %b.1, s32[4,32]{1,0:T(4,128)} %bm.1), custom_call_target="tpu_custom_call" | custom-call | tf_op jit(solution)/shard_map/exchange/pallas_call | solution.py:431
  175.0 6.6 %deliver.1 = bf16[64,4,128,128]{3,2,1,0:T(8,128)(2,1)} custom-call(bf16[64,4,128,128]{3,2,1,0:T(8,128)(2,1)} %bitcast.1), custom_call_target="tpu_custom_call" | custom-call | tf_op jit(solution)/shard_map/deliver/pallas_call | solution.py:467
